TPU v7x, 32 devices: a whole 2x2x4 slice. The times are simulated.
32 devices in a mesh: groups: 2 (over y), ctx: 4 (over z), head: 4 (over x, core).
Axes of the slice: x: 2, y: 2, z: 4, core: 2. Of those that a mesh axis runs over, the one named last changes fastest.
Arguments:
- queries: bfloat16 [8192, 3584], P(('groups', 'ctx'), 'head'), parts along dimension 0, may hold values from -13 to 13
- key_states: bfloat16 [8192, 512], P(('groups', 'ctx'), 'head'), parts along dimension 0, may hold values from -13 to 13
- value_states: bfloat16 [8192, 512], P(('groups', 'ctx'), 'head'), parts along dimension 0, may hold values from -6 to 6
- vertical: int32 [8, 2], P(('groups', 'head')), parts along dimension 0, may hold values from 0 to 31, as said below
- offsets: int32 [8, 4], P(('groups', 'head')), parts along dimension 0, may hold values from 0 to 960, as said below
Outputs:
- attended: bfloat16 [8192, 3584], P(('groups', 'ctx'), 'head'), parts along dimension 0
There are 2 independent parts, one for each index of `groups`. A program takes and returns all parts, laid end to end along the dimension named above; each array names one. Nothing has to cross between parts.
Inputs may be any that keep to these rules, and one draw needn't show every extreme that they name: `vertical`: each row lists 2 distinct blocks; the 1024 tokens of one ctx shard hold at most one block of a row. `offsets`: each row holds distinct multiples of 64; its first entry is 0 and its second is 960.
All inputs are finite; a program needn't handle non-finite values.
Results may differ from a plain program's by a relative error of at most 0.0043.
Values may be sent and summed in bfloat16 or wider, within the bound.
No kernel may reach another device: no remote copies, remote signals or barrier semaphores. Data moves between devices by JAX's collectives and lax.ppermute only.
A program may use at most 256 MiB of HBM per device.

v0:
```python
import jax
import jax.numpy as jnp
from jax import lax
from jax.sharding import PartitionSpec as P

BLOCK = 128
BAND = 64


def shifted(block, axis, distance):
    devices = range(lax.axis_size(axis))
    route = [(i - distance, i) for i in devices if i - distance in devices]
    return lax.ppermute(block, axis, route)


def attend(running, block_keys, block_values, visible, query_mat, scaling):
    run_max, run_sum, run_acc = running
    scores = (
        jnp.einsum("tgd,kd->tgk", query_mat, block_keys, preferred_element_type=jnp.float32)
        * scaling
    )
    masked = jnp.where(visible[:, None, :], scores, -1e30)
    new_max = jnp.maximum(run_max, jnp.max(masked, axis=-1))
    correct = jnp.exp(run_max - new_max)
    weights = jnp.where(visible[:, None, :], jnp.exp(masked - new_max[..., None]), 0.0)
    new_sum = run_sum * correct + jnp.sum(weights, axis=-1)
    rounded = weights.astype(jnp.bfloat16)
    new_acc = run_acc * correct[..., None] + jnp.einsum(
        "tgk,kd->tgd", rounded, block_values, preferred_element_type=jnp.float32
    )
    return (new_max, new_sum, new_acc)


def per_device(queries, key_states, value_states, vertical, offsets):
    tok_rows = queries.shape[0]
    head_dim = key_states.shape[1]
    group_size = queries.shape[1] // head_dim
    scaling = head_dim ** (-0.5)
    my_rank = lax.axis_index("ctx")
    first_pos = my_rank * tok_rows
    query_pos = first_pos + jnp.arange(tok_rows, dtype=jnp.int32)
    vert_list = vertical[0]
    slash_offs = offsets[0]
    query_mat = queries.reshape(tok_rows, group_size, head_dim)
    prev_keys, prev_values = shifted((key_states, value_states), "ctx", 1)
    window_keys = jnp.concatenate([prev_keys, key_states], 0)
    window_values = jnp.concatenate([prev_values, value_states], 0)
    window_pos = first_pos - tok_rows + jnp.arange(2 * tok_rows, dtype=jnp.int32)
    distance = query_pos[:, None] - window_pos[None, :]
    in_band = jnp.any(
        (distance[None] >= slash_offs[:, None, None])
        & (distance[None] < slash_offs[:, None, None] + BAND),
        axis=0,
    )
    in_vert = jnp.any((window_pos // BLOCK)[:, None] == vert_list[None, :], axis=1)
    window_mask = in_band & (window_pos >= 0)[None, :] & jnp.logical_not(in_vert)[None, :]
    start_state = (
        jnp.full((tok_rows, group_size), -1e30, jnp.float32),
        jnp.zeros((tok_rows, group_size), jnp.float32),
        jnp.zeros((tok_rows, group_size, head_dim), jnp.float32),
    )
    running = attend(start_state, window_keys, window_values, window_mask, query_mat, scaling)
    every_key, every_value = (
        lax.all_gather(key_states, "ctx", axis=0, tiled=True),
        lax.all_gather(value_states, "ctx", axis=0, tiled=True),
    )
    vert_keys = every_key.reshape(-1, BLOCK, head_dim)[vert_list].reshape(-1, head_dim)
    vert_values = every_value.reshape(-1, BLOCK, head_dim)[vert_list].reshape(-1, head_dim)
    vert_pos = (vert_list[:, None] * BLOCK + jnp.arange(BLOCK, dtype=jnp.int32)[None, :]).reshape(
        -1
    )
    running = attend(
        running, vert_keys, vert_values, vert_pos[None, :] <= query_pos[:, None], query_mat, scaling
    )
    run_max, run_sum, run_acc = running
    return (
        (run_acc / run_sum[..., None]).reshape(tok_rows, group_size * head_dim).astype(jnp.bfloat16)
    )


def solution(mesh):
    placed = (
        P(("groups", "ctx"), "head"),
        P(("groups", "ctx"), "head"),
        P(("groups", "ctx"), "head"),
        P(("groups", "head"), None),
        P(("groups", "head"), None),
    )
    return jax.shard_map(
        per_device,
        mesh=mesh,
        in_specs=placed,
        out_specs=P(("groups", "ctx"), "head"),
        check_vma=False,
    )
```

profile of v0, /device:TPU:0, one launch (start us, length us, event | category | flops | bytes accessed | tf_op | source)
XLA Modules:
  0.0 144.3 jit_solution(5798919444002945875)
XLA Ops:
  6.5 0.0 copy-start.2
  6.5 0.0 all-gather.3.cloned.1.call-start
  6.5 0.7 all-gather.3.cloned.1.call-update
  7.3 0.0 all-gather.5.cloned.1.call-start
  7.3 4.9 %collective-permute-start = (bf16[1024,128]{1,0:T(8,128)(2,1)}, bf16[1024,128]{1,0:T(8,128)(2,1)S(1)}, u32[]{:S(2)}, u32[]{:S(2)}) collective-permute-start(bf16[1024,128]{1,0:T(8,128)(2,1)} %param.6), channel_id=1, source_target_pairs={{0,4},{4,8},{8,12},{1,5},{5,9},{9,13},{2,6},{6,10},{10,14},{3,7},{... | collective-permute-start | bytes 786440 | tf_op jit(solution)/shard_map/ppermute | solution.py:13
  12.3 0.0 all-gather.5.cloned.1.call-update
  12.3 1.1 copy.26
  13.4 3.5 %collective-permute-start.1 = (bf16[1024,128]{0,1:T(8,128)(2,1)S(1)}, bf16[1024,128]{0,1:T(8,128)(2,1)S(1)}, u32[]{:S(2)}, u32[]{:S(2)}) collective-permute-start(bf16[1024,128]{0,1:T(8,128)(2,1)S(1)} %copy.26), channel_id=1, source_target_pairs={{0,4},{4,8},{8,12},{1,5},{5,9},{9,13},{2,6},{6,10},{10,14},{3,7},{... | collective-permute-start | bytes 786440 | tf_op jit(solution)/shard_map/ppermute | solution.py:13
  16.9 0.7 broadcast_multiply_fusion
  17.6 0.7 fusion.27
  18.2 0.7 broadcast_add_fusion
  18.9 0.8 compare_reduce_fusion
  19.7 0.1 add_bitcast_fusion
  19.7 0.6 broadcast_subtract_fusion
  20.4 0.0 copy-done.2
  20.4 10.3 %and_reduce_fusion = pred[1024,2048]{1,0:T(8,128)(4,1)S(1)} fusion(s32[1024,2048]{1,0:T(8,128)S(1)} %broadcast_subtract_fusion, s32[4]{0:T(128)S(1)} %broadcast_add_fusion, s32[4]{0:T(128)S(1)} %bitcast.64), kind=kLoop, calls=%fused_computation.7 | loop fusion | flops 31457280 | bytes 10485792 | tf_op jit(solution)/shard_map/reduce_or | solution.py:50
  30.6 0.0 copy-start.1
  30.6 2.9 %and_and_fusion = pred[1024,2048]{1,0:T(8,128)(4,1)} fusion(pred[1024,2048]{1,0:T(8,128)(4,1)S(1)} %and_reduce_fusion, pred[2048]{0:T(1024)(128)(4,1)S(1)} %not.7, pred[2048]{0:T(1024)(128)(4,1)S(1)} %fusion.25), kind=kLoop, calls=%fused_computation.10 | loop fusion | flops 4194304 | bytes 4198400 | tf_op jit(solution)/shard_map/and | solution.py:56
  33.5 5.3 %copy.23 = pred[1024,2048]{0,1:T(8,128)(4,1)S(1)} copy(pred[1024,2048]{1,0:T(8,128)(4,1)} %and_and_fusion) | data formatting | bytes 4194304 | tf_op jit(solution)/shard_map/and | solution.py:56
  38.9 3.8 %copy.24 = bf16[1024,896]{0,1:T(8,128)(2,1)} copy(bf16[1024,896]{1,0:T(8,128)(2,1)} %param.5) | data formatting | bytes 3670016 | tf_op args[0]
  42.7 0.2 broadcast_compare_fusion
  42.9 0.0 collective-permute-done
  42.9 0.0 copy-done.1
  42.9 24.5 %fusion = (f32[1024,7]{0,1:T(8,128)S(1)}, f32[2048,1024,7]{1,0,2:T(8,128)}) fusion(pred[1024,2048]{0,1:T(8,128)(4,1)S(1)} %copy.23, bf16[1024,7,128]{0,2,1:T(8,128)(2,1)} %bitcast.57, bf16[1024,128]{1,0:T(8,128)(2,1)S(1)} %copy-done.1, bf16[1024,128]{1,0:T(8,128)(2,1)S(1)} %collective-permute-done), kind=kOutput, calls=%fused_computation.4 | convolution fusion | flops 3803177984 | bytes 63205376 | tf_op jit(solution)/shard_map/tgd,kd->tgk/dot_general | solution.py:19
  67.4 0.0 all-gather.3.cloned.1.call-done
  67.4 1.8 %gather_fusion = bf16[2,128,128]{2,1,0:T(8,128)(2,1)S(1)} fusion(bf16[32,128,128]{2,1,0:T(8,128)(2,1)} %bitcast.62, s32[1024]{0:T(1024)S(1)} %pad_clamp_fusion), kind=kCustom, calls=%fused_computation | custom fusion | bytes 131080 | tf_op jit(solution)/shard_map/gather | solution.py:67
  69.2 3.3 %all-gather.5.cloned.1.call-done = bf16[4096,128]{1,0:T(8,128)(2,1)} async-done(((bf16[1024,128]{1,0:T(8,128)(2,1)}), bf16[4096,128]{1,0:T(8,128)(2,1)}) %all-gather.5.cloned.1.call-update) | async-done | bytes 1048592 | tf_op jit(solution)/shard_map/all_gather | solution.py:65
  72.6 1.8 %gather_fusion.1 = bf16[2,128,128]{2,1,0:T(8,128)(2,1)S(1)} fusion(bf16[32,128,128]{2,1,0:T(8,128)(2,1)} %bitcast.63, s32[1024]{0:T(1024)S(1)} %pad_clamp_fusion), kind=kCustom, calls=%fused_computation.1 | custom fusion | bytes 131080 | tf_op jit(solution)/shard_map/gather | solution.py:68
  74.4 6.0 %fusion.6 = (f32[1024,7]{0,1:T(8,128)S(1)}, f32[256,1024,7]{1,0,2:T(8,128)}) fusion(pred[1024,256]{0,1:T(8,128)(4,1)S(1)} %broadcast_compare_fusion, bf16[256,128,1]{1,0,2:T(8,128)(2,1)S(1)} %bitcast.60, bf16[1024,7,128]{0,2,1:T(8,128)(2,1)} %bitcast.58), kind=kOutput, calls=%fused_computation.13 | convolution fusion | flops 475259904 | bytes 9531392 | tf_op jit(solution)/shard_map/tgd,kd->tgk/dot_general | solution.py:19
  80.3 20.0 %fusion.1 = f32[1024,7]{0,1:T(8,128)S(1)} fusion(f32[2048,1024,7]{1,0,2:T(8,128)} %get-tuple-element.11, f32[1024,7]{0,1:T(8,128)S(1)} %get-tuple-element.9, pred[1024,2048]{0,1:T(8,128)(4,1)S(1)} %copy.23), kind=kLoop, calls=%fused_computation.5 | loop fusion | flops 73393152 | bytes 60874752 | tf_op jit(solution)/shard_map/reduce_sum | solution.py:26
  100.4 0.0 copy-start
  100.4 5.0 %fusion.7 = f32[1024,7]{0,1:T(8,128)S(1)} fusion(f32[256,1024,7]{1,0,2:T(8,128)} %get-tuple-element.13, f32[1024,7]{0,1:T(8,128)S(1)} %get-tuple-element.8, pred[1024,256]{0,1:T(8,128)(4,1)S(1)} %broadcast_compare_fusion), kind=kLoop, calls=%fused_computation.14 | loop fusion | flops 9167872 | bytes 7659520 | tf_op jit(solution)/shard_map/reduce_sum | solution.py:26
  105.4 0.1 copy-done
  105.5 2.4 %fusion.9 = f32[1024,7,128]{0,2,1:T(8,128)S(1)} fusion(bf16[256,128,1]{1,0,2:T(8,128)(2,1)S(1)} %bitcast.61, f32[256,1024,7]{1,0,2:T(8,128)S(1)} %copy-done, f32[1024,7]{0,1:T(8,128)S(1)} %get-tuple-element.8, pred[1024,256]{0,1:T(8,128)(4,1)S(1)} %broadcast_compare_fusion), kind=kOutput, calls=%fused_computation.17 | convolution fusion | flops 478937088 | bytes 11366400 | tf_op jit(solution)/shard_map/tgk,kd->tgd/dot_general | solution.py:28
  108.0 0.0 collective-permute-done.1
  108.0 25.6 %divide_convert_fusion = bf16[1024,7,128]{0,2,1:T(8,128)(2,1)} fusion(f32[1024,7,128]{0,2,1:T(8,128)S(1)} %fusion.9, f32[2048,1024,7]{1,0,2:T(8,128)} %get-tuple-element.11, f32[1024,7]{0,1:T(8,128)S(1)} %get-tuple-element.9, pred[1024,2048]{0,1:T(8,128)(4,1)S(1)} %copy.23, f32[1024,7]{0,1:T(8,128)S(1)} %get-tuple-element.5, ...), kind=kOutput, calls=%fused_computation.18 | convolution fusion | flops 3837132800 | bytes 66961408 | tf_op jit(solution)/shard_map/tgk,kd->tgd/dot_general | solution.py:28
  133.7 3.8 %copy.32 = bf16[1024,896]{1,0:T(8,128)(2,1)} copy(bf16[1024,896]{0,1:T(8,128)(2,1)} %bitcast.59) | data formatting | bytes 3670016 | tf_op jit(solution)/shard_map/convert_element_type | solution.py:77
  (7 shorter events, 0.1 us)
Async XLA Ops:
  6.5 13.8 %copy-start.2 = (s32[1,4]{1,0:T(1,128)S(1)}, s32[1,4]{1,0:T(1,128)}, u32[]{:S(2)}) copy-start(s32[1,4]{1,0:T(1,128)} %param.9) | copy-start | bytes 52
  6.5 60.9 %all-gather.3.cloned.1.call-start = ((), (), s32[]{:S(2)}) async-start(), calls=%async_computation | async-start | bytes 1310720 | tf_op jit(solution)/shard_map/all_gather | solution.py:64
  7.3 65.3 %all-gather.5.cloned.1.call-start = ((), (), s32[]{:S(2)}) async-start(), calls=%async_computation.1 | async-start | bytes 1310720 | tf_op jit(solution)/shard_map/all_gather | solution.py:65
  7.3 35.6 %collective-permute-start = (bf16[1024,128]{1,0:T(8,128)(2,1)}, bf16[1024,128]{1,0:T(8,128)(2,1)S(1)}, u32[]{:S(2)}, u32[]{:S(2)}) collective-permute-start(bf16[1024,128]{1,0:T(8,128)(2,1)} %param.6), channel_id=1, source_target_pairs={{0,4},{4,8},{8,12},{1,5},{5,9},{9,13},{2,6},{6,10},{10,14},{3,7},{... | collective-permute-start | bytes 786440 | tf_op jit(solution)/shard_map/ppermute | solution.py:13
  13.4 94.6 %collective-permute-start.1 = (bf16[1024,128]{0,1:T(8,128)(2,1)S(1)}, bf16[1024,128]{0,1:T(8,128)(2,1)S(1)}, u32[]{:S(2)}, u32[]{:S(2)}) collective-permute-start(bf16[1024,128]{0,1:T(8,128)(2,1)S(1)} %copy.26), channel_id=1, source_target_pairs={{0,4},{4,8},{8,12},{1,5},{5,9},{9,13},{2,6},{6,10},{10,14},{3,7},{... | collective-permute-start | bytes 786440 | tf_op jit(solution)/shard_map/ppermute | solution.py:13
  30.6 12.3 %copy-start.1 = (bf16[1024,128]{1,0:T(8,128)(2,1)S(1)}, bf16[1024,128]{1,0:T(8,128)(2,1)}, u32[]{:S(2)}) copy-start(bf16[1024,128]{1,0:T(8,128)(2,1)} %param.6) | copy-start | bytes 786436
  100.4 5.2 %copy-start = (f32[256,1024,7]{1,0,2:T(8,128)S(1)}, f32[256,1024,7]{1,0,2:T(8,128)}, u32[]{:S(2)}) copy-start(f32[256,1024,7]{1,0,2:T(8,128)} %get-tuple-element.13) | copy-start | bytes 22020100
Sparse Core Ops, SparseCore 0:
  8.9 31.6 all-gather.2
  42.2 30.3 all-gather.4
where the time goes:
time: 145 us; the launch traced here: 144 us
  matrix products  58.6 us (40%)
  other arithmetic  41.9 us (29%)
  local copies, waits for them, and re-layouts  17.7 us (12%)
  between operations  13.6 us (9%)
  starting transfers between devices  8.47 us (6%)
  waiting for transfers between devices  4.06 us (3%)
    dot_general x2, matrix products, attend(): jnp.einsum('tgd,kd->tgk', query_mat, block_keys, preferred_element_type=j...  30.5 us
    dot_general x2, matrix products, attend(): jnp.einsum('tgk,kd->tgd', rounded, block_values, preferred_element_type=j...  28.1 us
    reduce_sum x2, other arithmetic, attend(): new_sum = run_sum * correct + jnp.sum(weights, axis=-1)  25.1 us
    reduce_or x1, other arithmetic, per_device(): jnp.any((distance[None] >= slash_offs[:, None, None]) & (distance[None] <...  10.3 us
    ppermute x2, starting transfers between devices, shifted(): return lax.ppermute(block, axis, route)  8.43 us
    and x1, local copies, waits for them, and re-layouts, per_device(): in_band & (window_pos >= 0)[None, :] & jnp.logical_not(in_vert)[None, :]  5.35 us
    unnamed x8, local copies, waits for them, and re-layouts  5.02 us
    convert_element_type x1, local copies, waits for them, and re-layouts, per_device(): (run_acc / run_sum[..., None]).reshape(tok_rows, group_size * head_dim)  3.8 us
  transfers between devices with their start and end apart: 4, of which 1 were waited for; matrix products, arithmetic and copies ran while one was open for 61% of the time, Pallas kernels for 0%

commit v1 on v0

v1 whole, which is shorter than its diff:
```python
import functools
import math

import jax
import jax.numpy as jnp
from jax import lax
from jax.experimental import pallas as pl
from jax.experimental.pallas import tpu as pltpu
from jax.sharding import PartitionSpec as P

BLOCK = 128
BAND = 64
NEG = -1e30


def ring(block, axis, distance):
    size = lax.axis_size(axis)
    return lax.ppermute(block, axis, [(i, (i + distance) % size) for i in range(size)])


def listed_here(vertical, rank, per_shard):
    local = vertical[0] - rank * per_shard
    mine = (local >= 0) & (local < per_shard)
    return jnp.sum(jnp.where(mine, local, 0)) * BLOCK


def attention_kernel(offs, vert, q_hbm, k_own, v_own, k_prev, v_prev, *rest, heads, dim, unroll, direct):
    n_remote = len(rest) - 9
    remote, (o_hbm, q_buf, kw, vw, vk, vv, o_buf, sems, out_sems) = rest[:n_remote], rest[n_remote:]
    tok = k_own.shape[0]
    listed = vert.shape[1]
    bands = offs.shape[1]
    per_shard = tok // BLOCK
    steps = tok // BAND // unroll
    rows = unroll * BAND
    rank = lax.axis_index("ctx")
    scale = dim**-0.5 * math.log2(math.e)

    def fetch(src, dst, sem):
        return pltpu.make_async_copy(src, dst, sems.at[sem])

    loads = [
        fetch(k_own, kw.at[pl.ds(tok, tok), :], 0),
        fetch(k_prev, kw.at[pl.ds(0, tok), :], 1),
        fetch(v_own, vw.at[pl.ds(tok, tok), pl.ds(0, dim)], 2),
        fetch(v_prev, vw.at[pl.ds(0, tok), pl.ds(0, dim)], 3),
    ]
    for copy in loads:
        copy.start()
    q_sem = 4 + 2 * listed

    def q_copy(i):
        at = pl.ds(pl.multiple_of(i * rows, rows), rows)
        return fetch(q_hbm.at[at, :], q_buf.at[at, :], q_sem + i)

    for i in range(steps):
        q_copy(i).start()
    for v in range(listed):
        block = vert[0, v]
        owner = lax.div(block, per_shard)
        row = pl.multiple_of((block - owner * per_shard) * BLOCK, BLOCK)
        away = rank - owner
        k_dst, v_dst = vk.at[pl.ds(v * BLOCK, BLOCK), :], vv.at[pl.ds(v * BLOCK, BLOCK), pl.ds(0, dim)]
        sources = [(away <= 0, k_own.at[pl.ds(row, BLOCK), :], v_own.at[pl.ds(row, BLOCK), :])]
        sources += [(away == 1, k_prev.at[pl.ds(row, BLOCK), :], v_prev.at[pl.ds(row, BLOCK), :])]
        if direct:
            sources += [
                (away == 2 + i, r.at[pl.ds(0, BLOCK), :], r.at[pl.ds(BLOCK, BLOCK), :])
                for i, r in enumerate(remote)
            ]
        else:
            (r,) = remote
            at = pl.multiple_of(owner * 2 * BLOCK, BLOCK)
            sources += [(away >= 2, r.at[pl.ds(at, BLOCK), :], r.at[pl.ds(at + BLOCK, BLOCK), :])]
        for here, k_src, v_src in sources:

            @pl.when(here)
            def _():
                fetch(k_src, k_dst, 4 + 2 * v).start()
                fetch(v_src, v_dst, 5 + 2 * v).start()

    vw[:, dim:] = jnp.ones((2 * tok, dim), jnp.bfloat16)
    vv[:, dim:] = jnp.ones((listed * BLOCK, dim), jnp.bfloat16)
    r_at = lax.broadcasted_iota(jnp.int32, (BAND, BLOCK), 0)
    t_at = lax.broadcasted_iota(jnp.int32, (BAND, BLOCK), 1)
    band_bias = jnp.where((t_at > r_at) & (t_at <= r_at + BAND), 0.0, NEG)
    low = t_at < BAND
    for copy in loads:
        copy.wait()
    for v in range(listed):
        fetch(k_own.at[pl.ds(0, BLOCK), :], vk.at[pl.ds(v * BLOCK, BLOCK), :], 4 + 2 * v).wait()
        fetch(v_own.at[pl.ds(0, BLOCK), :], vv.at[pl.ds(v * BLOCK, BLOCK), pl.ds(0, dim)], 5 + 2 * v).wait()
    first = rank * (tok // BAND)

    def row_block(a):
        at = pl.ds(pl.multiple_of(a * BAND, BAND), BAND)
        q = jnp.concatenate([q_buf[at, h * dim : (h + 1) * dim] for h in range(heads)], 0)
        keys, values, biases = [], [], []
        for s in range(bands):
            back = lax.div(offs[0, s], BAND)
            start = pl.multiple_of(tok + (a - back - 1) * BAND, BAND)
            keys.append(kw[pl.ds(start, BLOCK), :])
            values.append(vw[pl.ds(start, BLOCK), :])
            column = []
            for half in (first + a - back - 1, first + a - back):
                hidden = half < 0
                for v in range(listed):
                    hidden = hidden | (lax.shift_right_arithmetic(half, 1) == vert[0, v])
                column.append(jnp.where(hidden, jnp.float32(NEG), jnp.float32(0)))
            biases.append(band_bias + jnp.where(low, column[0], column[1]))
        for v in range(listed):
            reach = (first + a) * BAND - vert[0, v] * BLOCK
            biases.append(jnp.where(t_at <= r_at + reach, 0.0, NEG))
        keys = jnp.concatenate(keys + [vk[...]], 0)
        values = jnp.concatenate(values + [vv[...]], 0)
        scores = lax.dot_general(q, keys, (((1,), (1,)), ((), ())), preferred_element_type=jnp.float32)
        parts = [
            scores[:, i * BLOCK : (i + 1) * BLOCK].reshape(heads, BAND, BLOCK) + bias[None]
            for i, bias in enumerate(biases)
        ]
        top = jnp.max(functools.reduce(jnp.maximum, parts), axis=-1, keepdims=True)
        weights = [
            jnp.exp2((part - top) * scale).reshape(heads * BAND, BLOCK).astype(jnp.bfloat16) for part in parts
        ]
        acc = jnp.dot(jnp.concatenate(weights, 1), values, preferred_element_type=jnp.float32)
        out = acc[:, :dim] / acc[:, dim:]
        for h in range(heads):
            o_buf[at, h * dim : (h + 1) * dim] = out[h * BAND : (h + 1) * BAND].astype(jnp.bfloat16)

    def o_copy(i):
        at = pl.ds(pl.multiple_of(i * rows, rows), rows)
        return pltpu.make_async_copy(o_buf.at[at, :], o_hbm.at[at, :], out_sems.at[i])

    def step(i, carry):
        q_copy(i).wait()
        for u in range(unroll):
            row_block(i * unroll + u)
        o_copy(i).start()
        return carry

    lax.fori_loop(0, steps, step, 0)
    for i in range(steps):
        o_copy(i).wait()


def per_device(queries, key_states, value_states, vertical, offsets):
    tok, dim = key_states.shape
    heads = queries.shape[1] // dim
    listed = vertical.shape[1]
    n_ctx = lax.axis_size("ctx")
    rank = lax.axis_index("ctx")
    k_prev, v_prev = ring(key_states, "ctx", 1), ring(value_states, "ctx", 1)
    row = listed_here(vertical, rank, tok // BLOCK)
    mine = jnp.concatenate(
        [lax.dynamic_slice_in_dim(x, row, BLOCK, 0) for x in (key_states, value_states)], 0
    )
    direct = n_ctx <= 4
    if direct:
        remote = [ring(mine, "ctx", d) for d in range(2, n_ctx)]
    else:
        remote = [lax.all_gather(mine, "ctx", axis=0, tiled=True)]
    unroll = 4
    steps = tok // BAND // unroll
    smem, hbm = pl.BlockSpec(memory_space=pltpu.SMEM), pl.BlockSpec(memory_space=pl.ANY)
    return pl.pallas_call(
        functools.partial(attention_kernel, heads=heads, dim=dim, unroll=unroll, direct=direct),
        out_shape=jax.ShapeDtypeStruct(queries.shape, jnp.bfloat16),
        in_specs=[smem] * 2 + [hbm] * (5 + len(remote)),
        out_specs=hbm,
        scratch_shapes=[
            pltpu.VMEM(queries.shape, jnp.bfloat16),
            pltpu.VMEM((2 * tok, dim), jnp.bfloat16),
            pltpu.VMEM((2 * tok, 2 * dim), jnp.bfloat16),
            pltpu.VMEM((listed * BLOCK, dim), jnp.bfloat16),
            pltpu.VMEM((listed * BLOCK, 2 * dim), jnp.bfloat16),
            pltpu.VMEM(queries.shape, jnp.bfloat16),
            pltpu.SemaphoreType.DMA((4 + 2 * listed + steps,)),
            pltpu.SemaphoreType.DMA((steps,)),
        ],
        compiler_params=pltpu.CompilerParams(vmem_limit_bytes=40 * 2**20),
    )(offsets, vertical, queries, key_states, value_states, k_prev, v_prev, *remote)


def solution(mesh):
    placed = (
        P(("groups", "ctx"), "head"),
        P(("groups", "ctx"), "head"),
        P(("groups", "ctx"), "head"),
        P(("groups", "head"), None),
        P(("groups", "head"), None),
    )
    return jax.shard_map(
        per_device,
        mesh=mesh,
        in_specs=placed,
        out_specs=P(("groups", "ctx"), "head"),
        check_vma=False,
    )
```

time: 145 us -> 38.3 us (0.26)
  matrix products: 58.6 us -> 0 us
  other arithmetic: 41.9 us -> 1.3 us
  between operations: 13.6 us -> 0.67 us
  Pallas kernels: 0 us -> 11.8 us
  local copies, waits for them, and re-layouts: 17.7 us -> 6.23 us
  waiting for transfers between devices: 4.06 us -> 10.2 us
    dot_general x4 -> x0, matrix products: 58.6 us -> none  [the longest x2 30.5 us: attend(): jnp.einsum('tgd,kd->tgk', query_mat, block_keys, preferred_element_type=j...]
    reduce_sum x2 -> x1, other arithmetic: 25.1 us -> 1.29 us  [listed_here(): return jnp.sum(jnp.where(mine, local, 0)) * BLOCK]
    pallas_call x0 -> x1, Pallas kernels: none -> 11.8 us  [per_device(): pl.pallas_call(functools.partial(attention_kernel, heads=heads, dim=dim,...]
    reduce_or x2 -> x0, other arithmetic: 11 us -> none  [the longest x1 10.3 us: per_device(): jnp.any((distance[None] >= slash_offs[:, None, None]) & (distance[None] <...]
    ppermute x2 -> x4, waiting for transfers between devices: 0.01 us -> 10.2 us  [ring(): lax.ppermute(block, axis, [(i, (i + distance) % size) for i in range(size)])]
    and x1 -> x0, local copies, waits for them, and re-layouts: 5.35 us -> none  [per_device(): in_band & (window_pos >= 0)[None, :] & jnp.logical_not(in_vert)[None, :]]
    convert_element_type x1 -> x0, local copies, waits for them, and re-layouts: 3.8 us -> none  [per_device(): (run_acc / run_sum[..., None]).reshape(tok_rows, group_size * head_dim)]
    gather x2 -> x0, local copies, waits for them, and re-layouts: 3.57 us -> none  [the longest x1 1.79 us: per_device(): every_key.reshape(-1, BLOCK, head_dim)[vert_list].reshape(-1, head_dim)]
  transfers between devices with their start and end apart: 4 -> 4, of which waited for: 1 -> 2; matrix products, arithmetic and copies ran while one was open for 61% -> 7% of each run, Pallas kernels for 0% -> 0%
where the time goes in v1:
time: 38.3 us; the launch traced here: 37.9 us
  Pallas kernels  11.8 us (31%)
  waiting for transfers between devices  10.2 us (27%)
  starting transfers between devices  7.68 us (20%)
  local copies, waits for them, and re-layouts  6.23 us (16%)
  other arithmetic  1.3 us (3%)
  between operations  0.67 us (2%)
    pallas_call x1, Pallas kernels, per_device(): pl.pallas_call(functools.partial(attention_kernel, heads=heads, dim=dim,...  11.8 us
    ppermute x4, waiting for transfers between devices, ring(): lax.ppermute(block, axis, [(i, (i + distance) % size) for i in range(size)])  10.2 us
    ppermute x4, starting transfers between devices, ring(): lax.ppermute(block, axis, [(i, (i + distance) % size) for i in range(size)])  7.68 us
    unnamed x10, local copies, waits for them, and re-layouts  4.71 us
    dynamic_slice x2, local copies, waits for them, and re-layouts, per_device(): lax.dynamic_slice_in_dim(x, row, BLOCK, 0)  1.53 us
    reduce_sum x1, other arithmetic, listed_here(): return jnp.sum(jnp.where(mine, local, 0)) * BLOCK  1.29 us
  transfers between devices with their start and end apart: 4, of which 2 were waited for; matrix products, arithmetic and copies ran while one was open for 7% of the time, Pallas kernels for 0%

profile of v1, /device:TPU:0, one launch (start us, length us, event | category | flops | bytes accessed | tf_op | source)
XLA Modules:
  0.0 37.9 jit_solution(12198536149422211175)
XLA Ops:
  0.0 3.0 %collective-permute-start = (bf16[1024,128]{1,0:T(8,128)(2,1)}, bf16[1024,128]{1,0:T(8,128)(2,1)S(1)}, u32[]{:S(2)}, u32[]{:S(2)}) collective-permute-start(bf16[1024,128]{1,0:T(8,128)(2,1)} %k_own.1), channel_id=1, source_target_pairs={{0,4},{4,8},{8,12},{12,0},{1,5},{5,9},{9,13},{13,1},{2,6},{6,10},{... | collective-permute-start | bytes 786440 | tf_op jit(solution)/shard_map/ppermute | solution.py:18
  3.0 1.6 %collective-permute-start.1 = (bf16[1024,128]{1,0:T(8,128)(2,1)}, bf16[1024,128]{1,0:T(8,128)(2,1)S(1)}, u32[]{:S(2)}, u32[]{:S(2)}) collective-permute-start(bf16[1024,128]{1,0:T(8,128)(2,1)} %v_own.1), channel_id=1, source_target_pairs={{0,4},{4,8},{8,12},{12,0},{1,5},{5,9},{9,13},{13,1},{2,6},{6,10},{... | collective-permute-start | bytes 786440 | tf_op jit(solution)/shard_map/ppermute | solution.py:18
  4.6 1.3 %fusion = s32[]{:T(128)} fusion(s32[1,2]{1,0:T(1,128)} %vert.1, s32[]{:T(128)S(6)} %mul.6), kind=kLoop, calls=%fused_computation.2 | loop fusion | flops 11 | bytes 16 | tf_op jit(solution)/shard_map/reduce_sum | solution.py:24
  6.6 0.8 %constant_dynamic-slice_fusion = bf16[128,128]{1,0:T(8,128)(2,1)S(1)} fusion(bf16[1024,128]{1,0:T(8,128)(2,1)} %v_own.1, s32[]{:T(128)S(6)} %select_n.9), kind=kLoop, calls=%fused_computation.3 | loop fusion | bytes 65540 | tf_op jit(solution)/shard_map/dynamic_slice | solution.py:155
  7.3 0.8 %constant_dynamic-slice_fusion.1 = bf16[128,128]{1,0:T(8,128)(2,1)S(1)} fusion(bf16[1024,128]{1,0:T(8,128)(2,1)} %k_own.1, s32[]{:T(128)S(6)} %select_n.9), kind=kLoop, calls=%fused_computation.4 | loop fusion | bytes 65540 | tf_op jit(solution)/shard_map/dynamic_slice | solution.py:155
  8.1 2.3 %collective-permute-start.3 = (bf16[256,128]{1,0:T(8,128)(2,1)S(1)}, bf16[256,128]{1,0:T(8,128)(2,1)S(1)}, u32[]{:S(2)}, u32[]{:S(2)}) collective-permute-start(bf16[256,128]{1,0:T(8,128)(2,1)S(1)} %pad_maximum_fusion), channel_id=1, source_target_pairs={{0,12},{4,0},{8,4},{12,8},{1,13},{5,1},{9,5},{13,9},{2,14},{6,2},{... | collective-permute-start | bytes 196616 | tf_op jit(solution)/shard_map/ppermute | solution.py:18
  10.4 0.8 %collective-permute-start.2 = (bf16[256,128]{1,0:T(8,128)(2,1)S(1)}, bf16[256,128]{1,0:T(8,128)(2,1)S(1)}, u32[]{:S(2)}, u32[]{:S(2)}) collective-permute-start(bf16[256,128]{1,0:T(8,128)(2,1)S(1)} %pad_maximum_fusion), channel_id=1, source_target_pairs={{0,8},{4,12},{8,0},{12,4},{1,9},{5,13},{9,1},{13,5},{2,10},{6,14},... | collective-permute-start | bytes 196616 | tf_op jit(solution)/shard_map/ppermute | solution.py:18
  11.2 7.4 %collective-permute-done.3.rest_1_ = bf16[256,128]{1,0:T(8,128)(2,1)S(1)} collective-permute-done((bf16[256,128]{1,0:T(8,128)(2,1)S(1)}, bf16[256,128]{1,0:T(8,128)(2,1)S(1)}, u32[]{:S(2)}, u32[]{:S(2)}) %collective-permute-start.3) | collective-permute-done | bytes 65568 | tf_op jit(solution)/shard_map/ppermute | solution.py:18
  18.6 2.8 %collective-permute-done.2.rest_0_ = bf16[256,128]{1,0:T(8,128)(2,1)S(1)} collective-permute-done((bf16[256,128]{1,0:T(8,128)(2,1)S(1)}, bf16[256,128]{1,0:T(8,128)(2,1)S(1)}, u32[]{:S(2)}, u32[]{:S(2)}) %collective-permute-start.2) | collective-permute-done | bytes 65568 | tf_op jit(solution)/shard_map/ppermute | solution.py:18
  21.4 0.0 collective-permute-done.k_prev
  21.4 0.0 collective-permute-done.1.v_prev
  21.4 0.0 copy-start
  21.4 1.5 %copy-done = bf16[1024,896]{1,0:T(8,128)(2,1)S(1)} copy-done((bf16[1024,896]{1,0:T(8,128)(2,1)S(1)}, bf16[1024,896]{1,0:T(8,128)(2,1)}, u32[]{:S(2)}) %copy-start) | copy-done | bytes 1835032
  22.9 0.0 copy-start.1
  22.9 0.9 %copy-done.1 = bf16[1024,128]{1,0:T(8,128)(2,1)S(1)} copy-done((bf16[1024,128]{1,0:T(8,128)(2,1)S(1)}, bf16[1024,128]{1,0:T(8,128)(2,1)}, u32[]{:S(2)}) %copy-start.1) | copy-done | bytes 262168
  23.9 0.0 copy-start.2
  23.9 0.9 %copy-done.2 = bf16[1024,128]{1,0:T(8,128)(2,1)S(1)} copy-done((bf16[1024,128]{1,0:T(8,128)(2,1)S(1)}, bf16[1024,128]{1,0:T(8,128)(2,1)}, u32[]{:S(2)}) %copy-start.2) | copy-done | bytes 262168
  24.8 0.0 copy-start.3
  24.8 0.7 %copy-done.3 = s32[1,4]{1,0:T(1,128)S(1)} copy-done((s32[1,4]{1,0:T(1,128)S(1)}, s32[1,4]{1,0:T(1,128)}, u32[]{:S(2)}) %copy-start.3) | copy-done | bytes 40
  25.5 0.0 copy-start.4
  25.5 0.7 %copy-done.4 = s32[1,2]{1,0:T(1,128)S(1)} copy-done((s32[1,2]{1,0:T(1,128)S(1)}, s32[1,2]{1,0:T(1,128)}, u32[]{:S(2)}) %copy-start.4) | copy-done | bytes 32
  26.1 11.8 %shard_map.55 = bf16[1024,896]{1,0:T(8,128)(2,1)} custom-call(s32[1,4]{1,0:T(1,128)S(1)} %copy-done.3, s32[1,2]{1,0:T(1,128)S(1)} %copy-done.4, bf16[1024,896]{1,0:T(8,128)(2,1)S(1)} %copy-done, bf16[1024,128]{1,0:T(8,128)(2,1)S(1)} %copy-done.1, bf16[1024,128]{1,0:T(8,128)(2,1)S(1)} %copy-done.2, bf16[1024,128]{1,0:T(8,128)(2,1)S(1)} %collective-permute-done.k_prev, ...), custom_call_target="tpu_custom_call" | custom-call | tf_op jit(solution)/shard_map/pallas_call | solution.py:165
  (1 shorter events, 0.0 us)
Async XLA Ops:
  0.0 21.4 %collective-permute-start = (bf16[1024,128]{1,0:T(8,128)(2,1)}, bf16[1024,128]{1,0:T(8,128)(2,1)S(1)}, u32[]{:S(2)}, u32[]{:S(2)}) collective-permute-start(bf16[1024,128]{1,0:T(8,128)(2,1)} %k_own.1), channel_id=1, source_target_pairs={{0,4},{4,8},{8,12},{12,0},{1,5},{5,9},{9,13},{13,1},{2,6},{6,10},{... | collective-permute-start | bytes 786440 | tf_op jit(solution)/shard_map/ppermute | solution.py:18
  3.0 18.4 %collective-permute-start.1 = (bf16[1024,128]{1,0:T(8,128)(2,1)}, bf16[1024,128]{1,0:T(8,128)(2,1)S(1)}, u32[]{:S(2)}, u32[]{:S(2)}) collective-permute-start(bf16[1024,128]{1,0:T(8,128)(2,1)} %v_own.1), channel_id=1, source_target_pairs={{0,4},{4,8},{8,12},{12,0},{1,5},{5,9},{9,13},{13,1},{2,6},{6,10},{... | collective-permute-start | bytes 786440 | tf_op jit(solution)/shard_map/ppermute | solution.py:18
  8.1 10.5 %collective-permute-start.3 = (bf16[256,128]{1,0:T(8,128)(2,1)S(1)}, bf16[256,128]{1,0:T(8,128)(2,1)S(1)}, u32[]{:S(2)}, u32[]{:S(2)}) collective-permute-start(bf16[256,128]{1,0:T(8,128)(2,1)S(1)} %pad_maximum_fusion), channel_id=1, source_target_pairs={{0,12},{4,0},{8,4},{12,8},{1,13},{5,1},{9,5},{13,9},{2,14},{6,2},{... | collective-permute-start | bytes 196616 | tf_op jit(solution)/shard_map/ppermute | solution.py:18
  10.4 11.0 %collective-permute-start.2 = (bf16[256,128]{1,0:T(8,128)(2,1)S(1)}, bf16[256,128]{1,0:T(8,128)(2,1)S(1)}, u32[]{:S(2)}, u32[]{:S(2)}) collective-permute-start(bf16[256,128]{1,0:T(8,128)(2,1)S(1)} %pad_maximum_fusion), channel_id=1, source_target_pairs={{0,8},{4,12},{8,0},{12,4},{1,9},{5,13},{9,1},{13,5},{2,10},{6,14},... | collective-permute-start | bytes 196616 | tf_op jit(solution)/shard_map/ppermute | solution.py:18
  21.4 1.5 %copy-start = (bf16[1024,896]{1,0:T(8,128)(2,1)S(1)}, bf16[1024,896]{1,0:T(8,128)(2,1)}, u32[]{:S(2)}) copy-start(bf16[1024,896]{1,0:T(8,128)(2,1)} %q_hbm.1) | copy-start | bytes 5505028
  22.9 0.9 %copy-start.1 = (bf16[1024,128]{1,0:T(8,128)(2,1)S(1)}, bf16[1024,128]{1,0:T(8,128)(2,1)}, u32[]{:S(2)}) copy-start(bf16[1024,128]{1,0:T(8,128)(2,1)} %k_own.1) | copy-start | bytes 786436
  23.9 0.9 %copy-start.2 = (bf16[1024,128]{1,0:T(8,128)(2,1)S(1)}, bf16[1024,128]{1,0:T(8,128)(2,1)}, u32[]{:S(2)}) copy-start(bf16[1024,128]{1,0:T(8,128)(2,1)} %v_own.1) | copy-start | bytes 786436
  24.8 0.7 %copy-start.3 = (s32[1,4]{1,0:T(1,128)S(1)}, s32[1,4]{1,0:T(1,128)}, u32[]{:S(2)}) copy-start(s32[1,4]{1,0:T(1,128)} %offs.1) | copy-start | bytes 52
  25.5 0.7 %copy-start.4 = (s32[1,2]{1,0:T(1,128)S(1)}, s32[1,2]{1,0:T(1,128)}, u32[]{:S(2)}) copy-start(s32[1,2]{1,0:T(1,128)} %vert.1) | copy-start | bytes 28

commit v2 on v0

v2 whole, which is shorter than its diff:
```python
import functools
import math

import jax
import jax.numpy as jnp
from jax import lax
from jax.experimental import pallas as pl
from jax.experimental.pallas import tpu as pltpu
from jax.sharding import PartitionSpec as P

BLOCK = 128
BAND = 64
CHUNK = 2
NEG = -1e30


def ring(block, axis, distance):
    size = lax.axis_size(axis)
    return lax.ppermute(block, axis, [(i, (i + distance) % size) for i in range(size)])


def line(block, axis, distance):
    size = lax.axis_size(axis)
    return lax.ppermute(block, axis, [(i, i + distance) for i in range(size - distance)])


def start_all(copies):
    for copy in copies:
        copy.start()


def wait_all(copies):
    for copy in copies:
        copy.wait()


def copies_of(pairs, sems):
    return [pltpu.make_async_copy(src, dst, sems.at[i]) for i, (src, dst) in enumerate(pairs)]


def block_at(block):
    return pl.ds(pl.multiple_of(block * BLOCK, BLOCK), BLOCK)


def listed_in(vert, shard, per_shard):
    block = jnp.int32(-1)
    for v in range(vert.shape[1]):
        local = vert[0, v] - shard * per_shard
        block = jnp.where((local >= 0) & (local < per_shard), local, block)
    return block


def early_block(vert, shard, per_shard):
    listed = listed_in(vert, shard, per_shard)
    half = per_shard // 2
    return jnp.where((listed >= 0) & (listed < half), listed, half - 1)


def late_block(early, j):
    return jnp.where(j >= early, j + 1, j)


def is_listed(half, vert):
    found = lax.shift_right_arithmetic(half, 1) == vert[0, 0]
    for v in range(1, vert.shape[1]):
        found = found | (lax.shift_right_arithmetic(half, 1) == vert[0, v])
    return found


def run_stages(bodies, after):
    order = [(0, 0)]
    for u in range(len(bodies)):
        order += [(u + 1, 0)] * (u + 1 < len(bodies)) + [(u, 1), (u, 2)]
    done = 0
    for u, _ in order:
        stores = next(bodies[u]) or []
        for ref, index, value in stores:
            ref[index] = value
        if stores:
            done += 1
            after(done)


def pick_kernel(vert_hbm, k_hbm, v_hbm, mine, early, vert, sems):
    load = copies_of([(vert_hbm, vert)], sems)
    start_all(load)
    tok = k_hbm.shape[0]
    per_shard = tok // BLOCK
    half = per_shard // 2
    rank = lax.axis_index("ctx")
    upper = pl.ds(tok // 2, tok // 2)
    pairs = []
    for i, x in enumerate((k_hbm, v_hbm)):
        pairs.append((x.at[upper, :], early.at[pl.ds(i * (half + 1) * BLOCK, half * BLOCK), :]))
    first = copies_of(pairs, sems.at[pl.ds(1, 2)])
    start_all(first)
    wait_all(load)
    listed = jnp.maximum(listed_in(vert, rank, per_shard), 0)
    moved = early_block(vert, rank, per_shard)
    pairs = []
    for i, x in enumerate((k_hbm, v_hbm)):
        pairs.append((x.at[block_at(listed), :], mine.at[pl.ds(i * BLOCK, BLOCK), :]))
        pairs.append((x.at[block_at(moved), :], early.at[pl.ds((i * (half + 1) + half) * BLOCK, BLOCK), :]))
    second = copies_of(pairs, sems.at[pl.ds(3, len(pairs))])
    start_all(second)
    wait_all(first + second)


def load_kernel(vert, offs_hbm, q_hbm, k_hbm, v_hbm, late, offs, q_ref, kw, vw, sems):
    tok = k_hbm.shape[0]
    per_shard = tok // BLOCK
    half = per_shard // 2
    own = pl.ds(tok, tok)
    moved = early_block(vert, lax.axis_index("ctx"), per_shard)
    pairs = [
        (x.at[block_at(late_block(moved, j)), :], late.at[pl.ds((i * (half - 1) + j) * BLOCK, BLOCK), :])
        for i, x in enumerate((k_hbm, v_hbm))
        for j in range(half - 1)
    ]
    pairs += [(offs_hbm, offs), (k_hbm, kw.at[own, :]), (v_hbm, vw.at[own, :]), (q_hbm, q_ref)]
    loads = copies_of(pairs, sems)
    start_all(loads)

    @pl.when(lax.axis_index("ctx") == 0)
    def _():
        zero = jnp.zeros((tok, k_hbm.shape[1]), jnp.bfloat16)
        kw[pl.ds(0, tok), :] = zero
        vw[pl.ds(0, tok), :] = zero

    wait_all(loads)


def attend_rows(groups, unroll, base, o_hbm, offs, vert, q_ref, kw, vw, vk, vv, o_buf, o_sems, heads, dim):
    tok = q_ref.shape[0]
    rows = heads * BAND
    listed = vert.shape[1]
    first = lax.axis_index("ctx") * (tok // BAND)
    scale = dim**-0.5 * math.log2(math.e)
    group = unroll * BAND
    r_at = lax.broadcasted_iota(jnp.int32, (BAND, BLOCK), 0)
    t_at = lax.broadcasted_iota(jnp.int32, (BAND, BLOCK), 1)
    mask = jnp.where((t_at > r_at) & (t_at <= r_at + BAND), 0.0, NEG)

    def row_block(a):
        keys, values, biases = [], [], []
        for s in range(offs.shape[1]):
            low = a - lax.div(offs[0, s], BAND) - 1
            at = pl.ds(pl.multiple_of(tok + low * BAND, BAND), BLOCK)
            keys.append(kw[at, :])
            values.append(vw[at, :])
            hidden = [(first + h < 0) | is_listed(first + h, vert) for h in (low, low + 1)]
            column = [jnp.where(h, jnp.float32(NEG), jnp.float32(0)) for h in hidden]
            biases.append(mask + jnp.where(t_at < BAND, column[0], column[1]))
        for v in range(listed):
            reach = (first + a) * BAND - vert[0, v] * BLOCK
            biases.append(jnp.where(t_at - r_at <= reach, 0.0, NEG))
        at = pl.ds(pl.multiple_of(a * BAND, BAND), BAND)
        q = jnp.concatenate([q_ref[at, h * dim : (h + 1) * dim] for h in range(heads)], 0)
        keys = jnp.concatenate(keys + [vk[...]], 0)
        scores = lax.dot_general(q, keys, (((1,), (1,)), ((), ())), preferred_element_type=jnp.float32)
        parts = [
            (scores[:, i * BLOCK : (i + 1) * BLOCK].reshape(heads, BAND, BLOCK) + bias[None]).reshape(rows, BLOCK)
            for i, bias in enumerate(biases)
        ]
        yield
        top = jnp.max(functools.reduce(jnp.maximum, parts), axis=-1, keepdims=True)
        rounded = jnp.concatenate([jnp.exp2((x - top) * scale).astype(jnp.bfloat16) for x in parts], 1)
        yield
        values = jnp.concatenate(values + [vv[...]], 0)
        values = jnp.concatenate([values, jnp.ones_like(values)], 1)
        acc = jnp.dot(rounded, values, preferred_element_type=jnp.float32)
        out = (acc[:, :dim] / acc[:, dim:]).astype(jnp.bfloat16)
        yield [(o_buf, (at, slice(h * dim, (h + 1) * dim)), out[h * BAND : (h + 1) * BAND]) for h in range(heads)]

    chunk = min(unroll, CHUNK)

    def out_copy(c):
        at = pl.ds(pl.multiple_of((base + c * chunk) * BAND, chunk * BAND), chunk * BAND)
        return pltpu.make_async_copy(o_buf.at[at, :], o_hbm.at[at, :], o_sems.at[c])

    def step(g, carry):
        def after(done):
            if done % chunk == 0:
                out_copy(g * (unroll // chunk) + done // chunk - 1).start()

        run_stages([row_block(base + g * unroll + u) for u in range(unroll)], after)
        return carry

    lax.fori_loop(0, groups, step, 0)
    for c in range(groups * unroll // chunk):
        out_copy(c).wait()


def load_listed(vert, rank, k_own, v_own, vk, vv, others):
    per_shard = k_own.shape[0] // BLOCK
    for v in range(vert.shape[1]):
        owner = lax.div(vert[0, v], per_shard)
        local = vert[0, v] - owner * per_shard
        dst = pl.ds(v * BLOCK, BLOCK)
        for here, k_src, v_src, k_block, v_block in [
            (rank <= owner, k_own, v_own, local, local),
            *others(owner, local),
        ]:

            @pl.when(here)
            def _():
                vk[dst, :] = k_src[block_at(k_block), :]
                vv[dst, :] = v_src[block_at(v_block), :]


def first_kernel(offs, vert, q_ref, k_win, v_win, o_hbm, vk, vv, o_buf, o_sems, *, heads, dim, unroll):
    tok = q_ref.shape[0]
    own = pl.ds(tok, tok)
    rank = lax.axis_index("ctx")

    @pl.when(rank == 0)
    def _():
        load_listed(vert, rank, k_win.at[own, :], v_win.at[own, :], vk, vv, lambda owner, local: [])
        attend_rows(
            tok // BAND // unroll, unroll, 0, o_hbm, offs, vert, q_ref, k_win, v_win, vk, vv, o_buf, o_sems, heads, dim
        )


def upper_kernel(offs, vert, q_ref, early, *refs, heads, dim, direct, unroll):
    remote, (o_hbm, kw, vw, vk, vv, o_buf, o_sems) = refs[:-10][::-1], refs[-7:]
    tok = q_ref.shape[0]
    per_shard = tok // BLOCK
    half = per_shard // 2
    rank = lax.axis_index("ctx")

    @pl.when(rank > 0)
    def _():
        moved = early_block(vert, rank - 1, per_shard)
        for i, w in enumerate((kw, vw)):
            at = i * (half + 1) * BLOCK
            w[pl.ds(half * BLOCK, half * BLOCK), :] = early[pl.ds(at, half * BLOCK), :]
            w[block_at(moved), :] = early[pl.ds(at + half * BLOCK, BLOCK), :]

        def others(owner, local):
            found = [(rank == owner + 1, kw, vw, local, local)]
            if direct:
                found += [(rank == owner + 2 + i, x, x, 0, 1) for i, x in enumerate(remote)]
            else:
                found.append((rank >= owner + 2, remote[0], remote[0], 2 * owner, 2 * owner + 1))
            return found

        own = pl.ds(tok, tok)
        load_listed(vert, rank, kw.at[own, :], vw.at[own, :], vk, vv, others)
        n = tok // BAND // 2
        attend_rows(n // unroll, unroll, n, o_hbm, offs, vert, q_ref, kw, vw, vk, vv, o_buf, o_sems, heads, dim)


def lower_kernel(offs, vert, q_ref, late, vk, vv, _o, _kw, _vw, o_hbm, kw, vw, o_buf, o_sems, *, heads, dim, unroll):
    tok = q_ref.shape[0]
    per_shard = tok // BLOCK
    half = per_shard // 2
    rank = lax.axis_index("ctx")

    @pl.when(rank > 0)
    def _():
        moved = early_block(vert, rank - 1, per_shard)
        for i, w in enumerate((kw, vw)):
            for j in range(half - 1):
                w[block_at(late_block(moved, j)), :] = late[pl.ds((i * (half - 1) + j) * BLOCK, BLOCK), :]
        n = tok // BAND // 2
        attend_rows(n // unroll, unroll, 0, o_hbm, offs, vert, q_ref, kw, vw, vk, vv, o_buf, o_sems, heads, dim)


def per_device(queries, key_states, value_states, vertical, offsets):
    tok, dim = key_states.shape
    heads = queries.shape[1] // dim
    listed = vertical.shape[1]
    n_ctx = lax.axis_size("ctx")
    half = tok // BLOCK // 2
    bf16 = jnp.bfloat16
    hbm = pl.BlockSpec(memory_space=pl.ANY)
    pinned = [
        pltpu.with_memory_space_constraint(x, pltpu.HBM)
        for x in (offsets, vertical, queries, key_states, value_states)
    ]
    vmem, smem = pl.BlockSpec(memory_space=pltpu.VMEM), pl.BlockSpec(memory_space=pltpu.SMEM)

    def params(flops, limit=24):
        return dict(
            compiler_params=pltpu.CompilerParams(vmem_limit_bytes=limit * 2**20),
            cost_estimate=pl.CostEstimate(flops=flops, bytes_accessed=2**20, transcendentals=0),
        )

    window, blocks = (2 * tok, dim), (listed * BLOCK, dim)
    mine, early, vert = pl.pallas_call(
        pick_kernel,
        out_shape=[pltpu.VMEM((2 * n * BLOCK, dim), bf16) for n in (1, half + 1)]
        + [pltpu.SMEM(vertical.shape, jnp.int32)],
        in_specs=[hbm] * 3,
        out_specs=[vmem, vmem, smem],
        scratch_shapes=[pltpu.SemaphoreType.DMA((7,))],
        **params(10**6),
    )(pinned[1], pinned[3], pinned[4])
    early = ring(early, "ctx", 1)
    direct = n_ctx <= 4
    if direct:
        remote = [line(mine, "ctx", d) for d in range(2, n_ctx)]
    else:
        remote = [lax.all_gather(mine, "ctx", axis=0, tiled=True)]
    late, offs, q, kw, vw = pl.pallas_call(
        load_kernel,
        out_shape=[
            pltpu.VMEM((2 * (half - 1) * BLOCK, dim), bf16),
            pltpu.SMEM(offsets.shape, jnp.int32),
            pltpu.VMEM(queries.shape, bf16),
            pltpu.VMEM(window, bf16),
            pltpu.VMEM(window, bf16),
        ],
        in_specs=[smem] + [hbm] * 4,
        out_specs=[vmem, smem, vmem, vmem, vmem],
        scratch_shapes=[pltpu.SemaphoreType.DMA((2 * half + 2,))],
        **params(10**6),
    )(vert, pinned[0], *pinned[2:])
    late = ring(late, "ctx", 1)
    unroll = (4, 8, 8) if listed <= 4 else (1, 1, 1)
    o_shape = jax.ShapeDtypeStruct(queries.shape, bf16)
    buffers = [pltpu.VMEM(queries.shape, bf16)]
    done = [pltpu.SemaphoreType.DMA((tok // BAND,))]
    out = pl.pallas_call(
        functools.partial(first_kernel, heads=heads, dim=dim, unroll=unroll[0]),
        out_shape=o_shape,
        in_specs=[smem, smem] + [vmem] * 3,
        out_specs=hbm,
        scratch_shapes=[pltpu.VMEM(blocks, bf16)] * 2 + buffers + done,
        **params(FLOPS[0]),
    )(offs, vert, q, kw, vw)
    n = 4 + len(remote)
    out, kw, vw, vk, vv = pl.pallas_call(
        functools.partial(upper_kernel, heads=heads, dim=dim, direct=direct, unroll=unroll[1]),
        out_shape=[o_shape] + [pltpu.VMEM(x, bf16) for x in (window, window, blocks, blocks)],
        in_specs=[smem, smem, vmem, vmem] + [vmem] * len(remote) + [hbm, vmem, vmem],
        out_specs=[hbm] + [vmem] * 4,
        input_output_aliases={n: 0, n + 1: 1, n + 2: 2},
        scratch_shapes=buffers + done,
        **params(FLOPS[1]),
    )(offs, vert, q, early, *remote[::-1], out, kw, vw)
    out, _, _ = pl.pallas_call(
        functools.partial(lower_kernel, heads=heads, dim=dim, unroll=unroll[2]),
        out_shape=[o_shape] + [pltpu.VMEM(window, bf16)] * 2,
        in_specs=[smem, smem] + [vmem] * 4 + [hbm, vmem, vmem],
        out_specs=[hbm] + [vmem] * 2,
        input_output_aliases={6: 0, 7: 1, 8: 2},
        scratch_shapes=buffers + done,
        **params(FLOPS[2]),
    )(offs, vert, q, late, vk, vv, out, kw, vw)
    return out


FLOPS = (10**6, 3 * 10**9, 10**6)


def solution(mesh):
    placed = (
        P(("groups", "ctx"), "head"),
        P(("groups", "ctx"), "head"),
        P(("groups", "ctx"), "head"),
        P(("groups", "head"), None),
        P(("groups", "head"), None),
    )
    return jax.shard_map(
        per_device,
        mesh=mesh,
        in_specs=placed,
        out_specs=P(("groups", "ctx"), "head"),
        check_vma=False,
    )
```

time: 145 us -> 25.6 us (0.18)
  the two profiles are of different devices: /device:TPU:0 before, /device:TPU:28 now
where the time goes in v2:
time: 25.6 us; the launch traced here: 25.3 us
  Pallas kernels  12.5 us (49%)
  starting transfers between devices  7.68 us (30%)
  waiting for transfers between devices  5.06 us (20%)
    ppermute x2, starting transfers between devices, ring(): lax.ppermute(block, axis, [(i, (i + distance) % size) for i in range(size)])  5.11 us
    ppermute x2, waiting for transfers between devices, line(): lax.ppermute(block, axis, [(i, i + distance) for i in range(size - distan...  5.05 us
    pallas_call x1, Pallas kernels, per_device(): pl.pallas_call(functools.partial(upper_kernel, heads=heads, dim=dim, dire...  4.47 us
    pallas_call x1, Pallas kernels, per_device(): pl.pallas_call(functools.partial(lower_kernel, heads=heads, dim=dim, unro...  4.44 us
    ppermute x2, starting transfers between devices, line(): lax.ppermute(block, axis, [(i, i + distance) for i in range(size - distan...  2.57 us
    pallas_call x1, Pallas kernels, per_device(): pl.pallas_call(load_kernel, out_shape=[pltpu.VMEM((2 * (half - 1) * BLOCK...  1.89 us
    pallas_call x1, Pallas kernels, per_device(): pl.pallas_call(pick_kernel, out_shape=[pltpu.VMEM((2 * n * BLOCK, dim), b...  1.57 us
  transfers between devices with their start and end apart: 4, of which 1 were waited for; matrix products, arithmetic and copies ran while one was open for 0% of the time, Pallas kernels for 26%

profile of v2, /device:TPU:28, one launch (start us, length us, event | category | flops | bytes accessed | tf_op | source)
XLA Modules:
  0.0 25.3 jit_solution(5027874764365541547)
XLA Ops:
  0.0 1.6 %shard_map.55 = (bf16[256,128]{1,0:T(8,128)(2,1)S(1)}, bf16[1280,128]{1,0:T(8,128)(2,1)S(1)}, s32[1,2]{1,0:T(1,128)S(4)}) custom-call(s32[1,2]{1,0:T(1,128)} %vert_hbm.1, bf16[1024,128]{1,0:T(8,128)(2,1)} %k_hbm.3, bf16[1024,128]{1,0:T(8,128)(2,1)} %v_hbm.3), custom_call_target="tpu_custom_call" | custom-call | flops 1000000 | bytes 1048576 | tf_op jit(solution)/shard_map/pallas_call | solution.py:290
  1.6 0.3 %collective-permute-start.1 = (bf16[1280,128]{1,0:T(8,128)(2,1)S(1)}, bf16[1280,128]{1,0:T(8,128)(2,1)S(1)}, u32[]{:S(2)}, u32[]{:S(2)}) collective-permute-start(bf16[1280,128]{1,0:T(8,128)(2,1)S(1)} %get-tuple-element.23), channel_id=1, source_target_pairs={{0,4},{4,8},{8,12},{12,0},{1,5},{5,9},{9,13},{13,1},{2,6},{6,10},{... | collective-permute-start | bytes 983048 | tf_op jit(solution)/shard_map/ppermute | solution.py:19
  1.9 1.3 %collective-permute-start.3 = (bf16[256,128]{1,0:T(8,128)(2,1)S(1)}, bf16[256,128]{1,0:T(8,128)(2,1)S(1)}, u32[]{:S(2)}, u32[]{:S(2)}) collective-permute-start(bf16[256,128]{1,0:T(8,128)(2,1)S(1)} %get-tuple-element.24), channel_id=1, source_target_pairs={{0,8},{4,12},{1,9},{5,13},{2,10},{6,14},{3,11},{7,15},{16,24},{20,... | collective-permute-start | bytes 196616 | tf_op jit(solution)/shard_map/ppermute | solution.py:24
  3.1 1.3 %collective-permute-start.2 = (bf16[256,128]{1,0:T(8,128)(2,1)S(1)}, bf16[256,128]{1,0:T(8,128)(2,1)S(1)}, u32[]{:S(2)}, u32[]{:S(2)}) collective-permute-start(bf16[256,128]{1,0:T(8,128)(2,1)S(1)} %get-tuple-element.24), channel_id=1, source_target_pairs={{0,12},{1,13},{2,14},{3,15},{16,28},{17,29},{18,30},{19,31}} | collective-permute-start | bytes 196616 | tf_op jit(solution)/shard_map/ppermute | solution.py:24
  4.4 1.9 %shard_map.56 = (bf16[768,128]{1,0:T(8,128)(2,1)S(1)}, s32[1,4]{1,0:T(1,128)S(4)}, bf16[1024,896]{1,0:T(8,128)(2,1)S(1)}, bf16[2048,128]{1,0:T(8,128)(2,1)S(1)}, bf16[2048,128]{1,0:T(8,128)(2,1)S(1)}) custom-call(s32[1,2]{1,0:T(1,128)S(4)} %get-tuple-element.19.vert, s32[1,4]{1,0:T(1,128)} %offs_hbm.1, bf16[1024,896]{1,0:T(8,128)(2,1)} %q_hbm.1, ...), custom_call_target="tpu_custom_call" | custom-call | flops 1000000 | bytes 1048576 | tf_op jit(solution)/shard_map/pallas_call | solution.py:305
  6.3 4.8 %collective-permute-start = (bf16[768,128]{1,0:T(8,128)(2,1)S(1)}, bf16[768,128]{1,0:T(8,128)(2,1)S(1)}, u32[]{:S(2)}, u32[]{:S(2)}) collective-permute-start(bf16[768,128]{1,0:T(8,128)(2,1)S(1)} %get-tuple-element.22), channel_id=1, source_target_pairs={{0,4},{4,8},{8,12},{12,0},{1,5},{5,9},{9,13},{13,1},{2,6},{6,10},{... | collective-permute-start | bytes 589832 | tf_op jit(solution)/shard_map/ppermute | solution.py:19
  11.2 0.1 shard_map.57.refs_2_
  11.3 5.0 %collective-permute-done.3.refs_1_ = bf16[256,128]{1,0:T(8,128)(2,1)S(1)} collective-permute-done((bf16[256,128]{1,0:T(8,128)(2,1)S(1)}, bf16[256,128]{1,0:T(8,128)(2,1)S(1)}, u32[]{:S(2)}, u32[]{:S(2)}) %collective-permute-start.3) | collective-permute-done | bytes 65568 | tf_op jit(solution)/shard_map/ppermute | solution.py:24
  16.4 0.0 collective-permute-done.2.refs_0_
  16.4 0.0 collective-permute-done.1.early
  16.4 4.5 %shard_map.58 = (bf16[1024,896]{1,0:T(8,128)(2,1)}, bf16[2048,128]{1,0:T(8,128)(2,1)S(1)}, bf16[2048,128]{1,0:T(8,128)(2,1)S(1)}, bf16[256,128]{1,0:T(8,128)(2,1)S(1)}, bf16[256,128]{1,0:T(8,128)(2,1)S(1)}) custom-call(s32[1,4]{1,0:T(1,128)S(4)} %get-tuple-element.20.offs, ...), custom_call_target="tpu_custom_call", output_to_operand_aliasing={{0}: (6, {}), {1}: (7, {}), {2}: (8, {})} | custom-call | flops 3000000000 | bytes 1048576 | tf_op jit(solution)/shard_map/pallas_call | solution.py:333
  20.9 0.0 collective-permute-done.late
  20.9 4.4 %shard_map.59 = (bf16[1024,896]{1,0:T(8,128)(2,1)}, bf16[2048,128]{1,0:T(8,128)(2,1)S(1)}, bf16[2048,128]{1,0:T(8,128)(2,1)S(1)}) custom-call(s32[1,4]{1,0:T(1,128)S(4)} %get-tuple-element.20.offs, s32[1,2]{1,0:T(1,128)S(4)} %get-tuple-element.19.vert, ...), custom_call_target="tpu_custom_call", output_to_operand_aliasing={{0}: (6, {}), {1}: (7, {}), {2}: (8, {})} | custom-call | flops 1000000 | bytes 1048576 | tf_op jit(solution)/shard_map/pallas_call | solution.py:342
Async XLA Ops:
  1.6 14.8 %collective-permute-start.1 = (bf16[1280,128]{1,0:T(8,128)(2,1)S(1)}, bf16[1280,128]{1,0:T(8,128)(2,1)S(1)}, u32[]{:S(2)}, u32[]{:S(2)}) collective-permute-start(bf16[1280,128]{1,0:T(8,128)(2,1)S(1)} %get-tuple-element.23), channel_id=1, source_target_pairs={{0,4},{4,8},{8,12},{12,0},{1,5},{5,9},{9,13},{13,1},{2,6},{6,10},{... | collective-permute-start | bytes 983048 | tf_op jit(solution)/shard_map/ppermute | solution.py:19
  1.9 14.5 %collective-permute-start.3 = (bf16[256,128]{1,0:T(8,128)(2,1)S(1)}, bf16[256,128]{1,0:T(8,128)(2,1)S(1)}, u32[]{:S(2)}, u32[]{:S(2)}) collective-permute-start(bf16[256,128]{1,0:T(8,128)(2,1)S(1)} %get-tuple-element.24), channel_id=1, source_target_pairs={{0,8},{4,12},{1,9},{5,13},{2,10},{6,14},{3,11},{7,15},{16,24},{20,... | collective-permute-start | bytes 196616 | tf_op jit(solution)/shard_map/ppermute | solution.py:24
  3.1 13.2 %collective-permute-start.2 = (bf16[256,128]{1,0:T(8,128)(2,1)S(1)}, bf16[256,128]{1,0:T(8,128)(2,1)S(1)}, u32[]{:S(2)}, u32[]{:S(2)}) collective-permute-start(bf16[256,128]{1,0:T(8,128)(2,1)S(1)} %get-tuple-element.24), channel_id=1, source_target_pairs={{0,12},{1,13},{2,14},{3,15},{16,28},{17,29},{18,30},{19,31}} | collective-permute-start | bytes 196616 | tf_op jit(solution)/shard_map/ppermute | solution.py:24
  6.3 14.5 %collective-permute-start = (bf16[768,128]{1,0:T(8,128)(2,1)S(1)}, bf16[768,128]{1,0:T(8,128)(2,1)S(1)}, u32[]{:S(2)}, u32[]{:S(2)}) collective-permute-start(bf16[768,128]{1,0:T(8,128)(2,1)S(1)} %get-tuple-element.22), channel_id=1, source_target_pairs={{0,4},{4,8},{8,12},{12,0},{1,5},{5,9},{9,13},{13,1},{2,6},{6,10},{... | collective-permute-start | bytes 589832 | tf_op jit(solution)/shard_map/ppermute | solution.py:19

commit v3 on v2

--- a/solution.py
+++ b/solution.py
@@ -81,52 +81,40 @@
             after(done)
 
 
-def pick_kernel(vert_hbm, k_hbm, v_hbm, mine, early, vert, sems):
-    load = copies_of([(vert_hbm, vert)], sems)
-    start_all(load)
-    tok = k_hbm.shape[0]
+def pick_kernel(vert_hbm, k_hbm, v_hbm, mine, early, vert, kw, vw, sems):
+    tok, dim = k_hbm.shape
+    own = pl.ds(tok, tok)
+    loads = copies_of([(vert_hbm, vert), (k_hbm, kw.at[own, :]), (v_hbm, vw.at[own, :])], sems)
+    start_all(loads)
+    rank = lax.axis_index("ctx")
+
+    @pl.when(rank == 0)
+    def _():
+        zero = jnp.zeros((tok, dim), jnp.bfloat16)
+        kw[pl.ds(0, tok), :] = zero
+        vw[pl.ds(0, tok), :] = zero
+
+    wait_all(loads)
     per_shard = tok // BLOCK
     half = per_shard // 2
-    rank = lax.axis_index("ctx")
-    upper = pl.ds(tok // 2, tok // 2)
-    pairs = []
-    for i, x in enumerate((k_hbm, v_hbm)):
-        pairs.append((x.at[upper, :], early.at[pl.ds(i * (half + 1) * BLOCK, half * BLOCK), :]))
-    first = copies_of(pairs, sems.at[pl.ds(1, 2)])
-    start_all(first)
-    wait_all(load)
     listed = jnp.maximum(listed_in(vert, rank, per_shard), 0)
     moved = early_block(vert, rank, per_shard)
-    pairs = []
-    for i, x in enumerate((k_hbm, v_hbm)):
-        pairs.append((x.at[block_at(listed), :], mine.at[pl.ds(i * BLOCK, BLOCK), :]))
-        pairs.append((x.at[block_at(moved), :], early.at[pl.ds((i * (half + 1) + half) * BLOCK, BLOCK), :]))
-    second = copies_of(pairs, sems.at[pl.ds(3, len(pairs))])
-    start_all(second)
-    wait_all(first + second)
-
-
-def load_kernel(vert, offs_hbm, q_hbm, k_hbm, v_hbm, late, offs, q_ref, kw, vw, sems):
-    tok = k_hbm.shape[0]
-    per_shard = tok // BLOCK
-    half = per_shard // 2
-    own = pl.ds(tok, tok)
+    for i, w in enumerate((kw, vw)):
+        at = i * (half + 1) * BLOCK
+        early[pl.ds(at, half * BLOCK), :] = w[pl.ds(tok + half * BLOCK, half * BLOCK), :]
+        early[pl.ds(at + half * BLOCK, BLOCK), :] = w[block_at(per_shard + moved), :]
+        mine[pl.ds(i * BLOCK, BLOCK), :] = w[block_at(per_shard + listed), :]
+
+
+def load_kernel(vert, offs_hbm, q_hbm, kw, vw, late, offs, q_ref, sems):
+    loads = copies_of([(offs_hbm, offs), (q_hbm, q_ref)], sems)
+    start_all(loads)
+    per_shard = kw.shape[0] // BLOCK // 2
+    half = per_shard // 2
     moved = early_block(vert, lax.axis_index("ctx"), per_shard)
-    pairs = [
-        (x.at[block_at(late_block(moved, j)), :], late.at[pl.ds((i * (half - 1) + j) * BLOCK, BLOCK), :])
-        for i, x in enumerate((k_hbm, v_hbm))
-        for j in range(half - 1)
-    ]
-    pairs += [(offs_hbm, offs), (k_hbm, kw.at[own, :]), (v_hbm, vw.at[own, :]), (q_hbm, q_ref)]
-    loads = copies_of(pairs, sems)
-    start_all(loads)
-
-    @pl.when(lax.axis_index("ctx") == 0)
-    def _():
-        zero = jnp.zeros((tok, k_hbm.shape[1]), jnp.bfloat16)
-        kw[pl.ds(0, tok), :] = zero
-        vw[pl.ds(0, tok), :] = zero
-
+    for i, w in enumerate((kw, vw)):
+        for j in range(half - 1):
+            late[pl.ds((i * (half - 1) + j) * BLOCK, BLOCK), :] = w[block_at(per_shard + late_block(moved, j)), :]
     wait_all(loads)
 
 
@@ -287,13 +275,14 @@
         )
 
     window, blocks = (2 * tok, dim), (listed * BLOCK, dim)
-    mine, early, vert = pl.pallas_call(
+    mine, early, vert, kw, vw = pl.pallas_call(
         pick_kernel,
         out_shape=[pltpu.VMEM((2 * n * BLOCK, dim), bf16) for n in (1, half + 1)]
-        + [pltpu.SMEM(vertical.shape, jnp.int32)],
+        + [pltpu.SMEM(vertical.shape, jnp.int32)]
+        + [pltpu.VMEM(window, bf16)] * 2,
         in_specs=[hbm] * 3,
-        out_specs=[vmem, vmem, smem],
-        scratch_shapes=[pltpu.SemaphoreType.DMA((7,))],
+        out_specs=[vmem, vmem, smem, vmem, vmem],
+        scratch_shapes=[pltpu.SemaphoreType.DMA((3,))],
         **params(10**6),
     )(pinned[1], pinned[3], pinned[4])
     early = ring(early, "ctx", 1)
@@ -302,20 +291,18 @@
         remote = [line(mine, "ctx", d) for d in range(2, n_ctx)]
     else:
         remote = [lax.all_gather(mine, "ctx", axis=0, tiled=True)]
-    late, offs, q, kw, vw = pl.pallas_call(
+    late, offs, q = pl.pallas_call(
         load_kernel,
         out_shape=[
             pltpu.VMEM((2 * (half - 1) * BLOCK, dim), bf16),
             pltpu.SMEM(offsets.shape, jnp.int32),
             pltpu.VMEM(queries.shape, bf16),
-            pltpu.VMEM(window, bf16),
-            pltpu.VMEM(window, bf16),
         ],
-        in_specs=[smem] + [hbm] * 4,
-        out_specs=[vmem, smem, vmem, vmem, vmem],
-        scratch_shapes=[pltpu.SemaphoreType.DMA((2 * half + 2,))],
+        in_specs=[smem, hbm, hbm, vmem, vmem],
+        out_specs=[vmem, smem, vmem],
+        scratch_shapes=[pltpu.SemaphoreType.DMA((2,))],
         **params(10**6),
-    )(vert, pinned[0], *pinned[2:])
+    )(vert, pinned[0], pinned[2], kw, vw)
     late = ring(late, "ctx", 1)
     unroll = (4, 8, 8) if listed <= 4 else (1, 1, 1)
     o_shape = jax.ShapeDtypeStruct(queries.shape, bf16)

time: 25.6 us -> 25 us (0.977)
  Pallas kernels: 12.5 us -> 11.7 us
  waiting for transfers between devices: 5.06 us -> 5.38 us
    pallas_call x1, Pallas kernels: 1.57 us -> 1.08 us  [per_device(): pl.pallas_call(pick_kernel, out_shape=[pltpu.VMEM((2 * n * BLOCK, dim), b...]
    pallas_call x1, Pallas kernels: 1.89 us -> 1.52 us  [per_device(): pl.pallas_call(load_kernel, out_shape=[pltpu.VMEM((2 * (half - 1) * BLOCK...]
    ppermute x2, waiting for transfers between devices: 5.05 us -> 5.38 us  [line(): lax.ppermute(block, axis, [(i, i + distance) for i in range(size - distan...]
  transfers between devices with their start and end apart: 4 -> 4, of which waited for: 1 -> 1; matrix products, arithmetic and copies ran while one was open for 0% -> 0% of each run, Pallas kernels for 26% -> 25%
where the time goes in v3:
time: 25 us; the launch traced here: 24.8 us
  Pallas kernels  11.7 us (47%)
  starting transfers between devices  7.68 us (31%)
  waiting for transfers between devices  5.38 us (22%)
    ppermute x2, waiting for transfers between devices, line(): lax.ppermute(block, axis, [(i, i + distance) for i in range(size - distan...  5.38 us
    ppermute x2, starting transfers between devices, ring(): lax.ppermute(block, axis, [(i, (i + distance) % size) for i in range(size)])  5.11 us
    pallas_call x1, Pallas kernels, per_device(): pl.pallas_call(functools.partial(upper_kernel, heads=heads, dim=dim, dire...  4.47 us
    pallas_call x1, Pallas kernels, per_device(): pl.pallas_call(functools.partial(lower_kernel, heads=heads, dim=dim, unro...  4.43 us
    ppermute x2, starting transfers between devices, line(): lax.ppermute(block, axis, [(i, i + distance) for i in range(size - distan...  2.57 us
    pallas_call x1, Pallas kernels, per_device(): pl.pallas_call(load_kernel, out_shape=[pltpu.VMEM((2 * (half - 1) * BLOCK...  1.52 us
    pallas_call x1, Pallas kernels, per_device(): pl.pallas_call(pick_kernel, out_shape=[pltpu.VMEM((2 * n * BLOCK, dim), b...  1.08 us
  transfers between devices with their start and end apart: 4, of which 1 were waited for; matrix products, arithmetic and copies ran while one was open for 0% of the time, Pallas kernels for 25%

profile of v3, /device:TPU:28, one launch (start us, length us, event | category | flops | bytes accessed | tf_op | source)
XLA Modules:
  0.0 24.8 jit_solution(17241421613304262371)
XLA Ops:
  0.0 1.1 %shard_map.55 = (bf16[256,128]{1,0:T(8,128)(2,1)S(1)}, bf16[1280,128]{1,0:T(8,128)(2,1)S(1)}, s32[1,2]{1,0:T(1,128)S(4)}, bf16[2048,128]{1,0:T(8,128)(2,1)S(1)}, bf16[2048,128]{1,0:T(8,128)(2,1)S(1)}) custom-call(s32[1,2]{1,0:T(1,128)} %vert_hbm.1, bf16[1024,128]{1,0:T(8,128)(2,1)} %k_hbm.1, bf16[1024,128]{1,0:T(8,128)(2,1)} %v_hbm.1), custom_call_target="tpu_custom_call" | custom-call | flops 1000000 | bytes 1048576 | tf_op jit(solution)/shard_map/pallas_call | solution.py:278
  1.1 0.3 %collective-permute-start.1 = (bf16[1280,128]{1,0:T(8,128)(2,1)S(1)}, bf16[1280,128]{1,0:T(8,128)(2,1)S(1)}, u32[]{:S(2)}, u32[]{:S(2)}) collective-permute-start(bf16[1280,128]{1,0:T(8,128)(2,1)S(1)} %get-tuple-element.25), channel_id=1, source_target_pairs={{0,4},{4,8},{8,12},{12,0},{1,5},{5,9},{9,13},{13,1},{2,6},{6,10},{... | collective-permute-start | bytes 983048 | tf_op jit(solution)/shard_map/ppermute | solution.py:19
  1.4 1.3 %collective-permute-start.3 = (bf16[256,128]{1,0:T(8,128)(2,1)S(1)}, bf16[256,128]{1,0:T(8,128)(2,1)S(1)}, u32[]{:S(2)}, u32[]{:S(2)}) collective-permute-start(bf16[256,128]{1,0:T(8,128)(2,1)S(1)} %get-tuple-element.26), channel_id=1, source_target_pairs={{0,8},{4,12},{1,9},{5,13},{2,10},{6,14},{3,11},{7,15},{16,24},{20,... | collective-permute-start | bytes 196616 | tf_op jit(solution)/shard_map/ppermute | solution.py:24
  2.7 1.3 %collective-permute-start.2 = (bf16[256,128]{1,0:T(8,128)(2,1)S(1)}, bf16[256,128]{1,0:T(8,128)(2,1)S(1)}, u32[]{:S(2)}, u32[]{:S(2)}) collective-permute-start(bf16[256,128]{1,0:T(8,128)(2,1)S(1)} %get-tuple-element.26), channel_id=1, source_target_pairs={{0,12},{1,13},{2,14},{3,15},{16,28},{17,29},{18,30},{19,31}} | collective-permute-start | bytes 196616 | tf_op jit(solution)/shard_map/ppermute | solution.py:24
  4.0 1.5 %shard_map.56 = (bf16[768,128]{1,0:T(8,128)(2,1)S(1)}, s32[1,4]{1,0:T(1,128)S(4)}, bf16[1024,896]{1,0:T(8,128)(2,1)S(1)}) custom-call(s32[1,2]{1,0:T(1,128)S(4)} %get-tuple-element.19.vert, s32[1,4]{1,0:T(1,128)} %offs_hbm.1, bf16[1024,896]{1,0:T(8,128)(2,1)} %q_hbm.1, bf16[2048,128]{1,0:T(8,128)(2,1)S(1)} %get-tuple-element.20.kw.k_win.refs_3_, ...), custom_call_target="tpu_custom_call" | custom-call | flops 1000000 | bytes 1048576 | tf_op jit(solution)/shard_map/pallas_call | solution.py:294
  5.5 4.8 %collective-permute-start = (bf16[768,128]{1,0:T(8,128)(2,1)S(1)}, bf16[768,128]{1,0:T(8,128)(2,1)S(1)}, u32[]{:S(2)}, u32[]{:S(2)}) collective-permute-start(bf16[768,128]{1,0:T(8,128)(2,1)S(1)} %get-tuple-element.24), channel_id=1, source_target_pairs={{0,4},{4,8},{8,12},{12,0},{1,5},{5,9},{9,13},{13,1},{2,6},{6,10},{... | collective-permute-start | bytes 589832 | tf_op jit(solution)/shard_map/ppermute | solution.py:19
  10.3 0.1 shard_map.57.refs_2_
  10.5 5.4 %collective-permute-done.3.refs_1_ = bf16[256,128]{1,0:T(8,128)(2,1)S(1)} collective-permute-done((bf16[256,128]{1,0:T(8,128)(2,1)S(1)}, bf16[256,128]{1,0:T(8,128)(2,1)S(1)}, u32[]{:S(2)}, u32[]{:S(2)}) %collective-permute-start.3) | collective-permute-done | bytes 65568 | tf_op jit(solution)/shard_map/ppermute | solution.py:24
  15.8 0.0 collective-permute-done.2.refs_0_
  15.8 0.0 collective-permute-done.1.early
  15.8 4.5 %shard_map.58 = (bf16[1024,896]{1,0:T(8,128)(2,1)}, bf16[2048,128]{1,0:T(8,128)(2,1)S(1)}, bf16[2048,128]{1,0:T(8,128)(2,1)S(1)}, bf16[256,128]{1,0:T(8,128)(2,1)S(1)}, bf16[256,128]{1,0:T(8,128)(2,1)S(1)}) custom-call(s32[1,4]{1,0:T(1,128)S(4)} %get-tuple-element.22.offs, ...), custom_call_target="tpu_custom_call", output_to_operand_aliasing={{0}: (6, {}), {1}: (7, {}), {2}: (8, {})} | custom-call | flops 3000000000 | bytes 1048576 | tf_op jit(solution)/shard_map/pallas_call | solution.py:320
  20.3 0.0 collective-permute-done.late
  20.3 4.4 %shard_map.59 = (bf16[1024,896]{1,0:T(8,128)(2,1)}, bf16[2048,128]{1,0:T(8,128)(2,1)S(1)}, bf16[2048,128]{1,0:T(8,128)(2,1)S(1)}) custom-call(s32[1,4]{1,0:T(1,128)S(4)} %get-tuple-element.22.offs, s32[1,2]{1,0:T(1,128)S(4)} %get-tuple-element.19.vert, ...), custom_call_target="tpu_custom_call", output_to_operand_aliasing={{0}: (6, {}), {1}: (7, {}), {2}: (8, {})} | custom-call | flops 1000000 | bytes 1048576 | tf_op jit(solution)/shard_map/pallas_call | solution.py:329
Async XLA Ops:
  1.1 14.8 %collective-permute-start.1 = (bf16[1280,128]{1,0:T(8,128)(2,1)S(1)}, bf16[1280,128]{1,0:T(8,128)(2,1)S(1)}, u32[]{:S(2)}, u32[]{:S(2)}) collective-permute-start(bf16[1280,128]{1,0:T(8,128)(2,1)S(1)} %get-tuple-element.25), channel_id=1, source_target_pairs={{0,4},{4,8},{8,12},{12,0},{1,5},{5,9},{9,13},{13,1},{2,6},{6,10},{... | collective-permute-start | bytes 983048 | tf_op jit(solution)/shard_map/ppermute | solution.py:19
  1.4 14.5 %collective-permute-start.3 = (bf16[256,128]{1,0:T(8,128)(2,1)S(1)}, bf16[256,128]{1,0:T(8,128)(2,1)S(1)}, u32[]{:S(2)}, u32[]{:S(2)}) collective-permute-start(bf16[256,128]{1,0:T(8,128)(2,1)S(1)} %get-tuple-element.26), channel_id=1, source_target_pairs={{0,8},{4,12},{1,9},{5,13},{2,10},{6,14},{3,11},{7,15},{16,24},{20,... | collective-permute-start | bytes 196616 | tf_op jit(solution)/shard_map/ppermute | solution.py:24
  2.7 13.2 %collective-permute-start.2 = (bf16[256,128]{1,0:T(8,128)(2,1)S(1)}, bf16[256,128]{1,0:T(8,128)(2,1)S(1)}, u32[]{:S(2)}, u32[]{:S(2)}) collective-permute-start(bf16[256,128]{1,0:T(8,128)(2,1)S(1)} %get-tuple-element.26), channel_id=1, source_target_pairs={{0,12},{1,13},{2,14},{3,15},{16,28},{17,29},{18,30},{19,31}} | collective-permute-start | bytes 196616 | tf_op jit(solution)/shard_map/ppermute | solution.py:24
  5.5 14.8 %collective-permute-start = (bf16[768,128]{1,0:T(8,128)(2,1)S(1)}, bf16[768,128]{1,0:T(8,128)(2,1)S(1)}, u32[]{:S(2)}, u32[]{:S(2)}) collective-permute-start(bf16[768,128]{1,0:T(8,128)(2,1)S(1)} %get-tuple-element.24), channel_id=1, source_target_pairs={{0,4},{4,8},{8,12},{12,0},{1,5},{5,9},{9,13},{13,1},{2,6},{6,10},{... | collective-permute-start | bytes 589832 | tf_op jit(solution)/shard_map/ppermute | solution.py:19

commit v4 on v3

--- a/solution.py
+++ b/solution.py
@@ -120,8 +120,8 @@
 
 def attend_rows(groups, unroll, base, o_hbm, offs, vert, q_ref, kw, vw, vk, vv, o_buf, o_sems, heads, dim):
     tok = q_ref.shape[0]
-    rows = heads * BAND
     listed = vert.shape[1]
+    parts_of = (range(0, (heads + 1) // 2), range((heads + 1) // 2, heads))
     first = lax.axis_index("ctx") * (tok // BAND)
     scale = dim**-0.5 * math.log2(math.e)
     group = unroll * BAND
@@ -129,7 +129,8 @@
     t_at = lax.broadcasted_iota(jnp.int32, (BAND, BLOCK), 1)
     mask = jnp.where((t_at > r_at) & (t_at <= r_at + BAND), 0.0, NEG)
 
-    def row_block(a):
+    def row_block(a, some):
+        rows = len(some) * BAND
         keys, values, biases = [], [], []
         for s in range(offs.shape[1]):
             low = a - lax.div(offs[0, s], BAND) - 1
@@ -143,11 +144,11 @@
             reach = (first + a) * BAND - vert[0, v] * BLOCK
             biases.append(jnp.where(t_at - r_at <= reach, 0.0, NEG))
         at = pl.ds(pl.multiple_of(a * BAND, BAND), BAND)
-        q = jnp.concatenate([q_ref[at, h * dim : (h + 1) * dim] for h in range(heads)], 0)
+        q = jnp.concatenate([q_ref[at, h * dim : (h + 1) * dim] for h in some], 0)
         keys = jnp.concatenate(keys + [vk[...]], 0)
         scores = lax.dot_general(q, keys, (((1,), (1,)), ((), ())), preferred_element_type=jnp.float32)
         parts = [
-            (scores[:, i * BLOCK : (i + 1) * BLOCK].reshape(heads, BAND, BLOCK) + bias[None]).reshape(rows, BLOCK)
+            (scores[:, i * BLOCK : (i + 1) * BLOCK].reshape(len(some), BAND, BLOCK) + bias[None]).reshape(rows, BLOCK)
             for i, bias in enumerate(biases)
         ]
         yield
@@ -158,7 +159,7 @@
         values = jnp.concatenate([values, jnp.ones_like(values)], 1)
         acc = jnp.dot(rounded, values, preferred_element_type=jnp.float32)
         out = (acc[:, :dim] / acc[:, dim:]).astype(jnp.bfloat16)
-        yield [(o_buf, (at, slice(h * dim, (h + 1) * dim)), out[h * BAND : (h + 1) * BAND]) for h in range(heads)]
+        yield [(o_buf, (at, slice(h * dim, (h + 1) * dim)), out[i * BAND : (i + 1) * BAND]) for i, h in enumerate(some)]
 
     chunk = min(unroll, CHUNK)
 
@@ -168,10 +169,10 @@
 
     def step(g, carry):
         def after(done):
-            if done % chunk == 0:
-                out_copy(g * (unroll // chunk) + done // chunk - 1).start()
-
-        run_stages([row_block(base + g * unroll + u) for u in range(unroll)], after)
+            if done % (2 * chunk) == 0:
+                out_copy(g * (unroll // chunk) + done // (2 * chunk) - 1).start()
+
+        run_stages([row_block(base + g * unroll + u, some) for u in range(unroll) for some in parts_of], after)
         return carry
 
     lax.fori_loop(0, groups, step, 0)

time: 25 us -> 24.8 us (level)
  no operation moved by 1% of the time
where the time goes in v4:
time: 24.8 us; the launch traced here: 24.6 us
  Pallas kernels  11.5 us (46%)
  starting transfers between devices  7.68 us (31%)
  waiting for transfers between devices  5.38 us (22%)
    ppermute x2, waiting for transfers between devices, line(): lax.ppermute(block, axis, [(i, i + distance) for i in range(size - distan...  5.38 us
    ppermute x2, starting transfers between devices, ring(): lax.ppermute(block, axis, [(i, (i + distance) % size) for i in range(size)])  5.11 us
    pallas_call x1, Pallas kernels, per_device(): pl.pallas_call(functools.partial(upper_kernel, heads=heads, dim=dim, dire...  4.36 us
    pallas_call x1, Pallas kernels, per_device(): pl.pallas_call(functools.partial(lower_kernel, heads=heads, dim=dim, unro...  4.34 us
    ppermute x2, starting transfers between devices, line(): lax.ppermute(block, axis, [(i, i + distance) for i in range(size - distan...  2.57 us
    pallas_call x1, Pallas kernels, per_device(): pl.pallas_call(load_kernel, out_shape=[pltpu.VMEM((2 * (half - 1) * BLOCK...  1.52 us
    pallas_call x1, Pallas kernels, per_device(): pl.pallas_call(pick_kernel, out_shape=[pltpu.VMEM((2 * n * BLOCK, dim), b...  1.08 us
  transfers between devices with their start and end apart: 4, of which 1 were waited for; matrix products, arithmetic and copies ran while one was open for 0% of the time, Pallas kernels for 25%

profile of v4, /device:TPU:28, one launch (start us, length us, event | category | flops | bytes accessed | tf_op | source)
XLA Modules:
  0.0 24.6 jit_solution(6003000549530061634)
XLA Ops:
  0.0 1.1 %shard_map.55 = (bf16[256,128]{1,0:T(8,128)(2,1)S(1)}, bf16[1280,128]{1,0:T(8,128)(2,1)S(1)}, s32[1,2]{1,0:T(1,128)S(4)}, bf16[2048,128]{1,0:T(8,128)(2,1)S(1)}, bf16[2048,128]{1,0:T(8,128)(2,1)S(1)}) custom-call(s32[1,2]{1,0:T(1,128)} %vert_hbm.1, bf16[1024,128]{1,0:T(8,128)(2,1)} %k_hbm.1, bf16[1024,128]{1,0:T(8,128)(2,1)} %v_hbm.1), custom_call_target="tpu_custom_call" | custom-call | flops 1000000 | bytes 1048576 | tf_op jit(solution)/shard_map/pallas_call | solution.py:279
  1.1 0.3 %collective-permute-start.1 = (bf16[1280,128]{1,0:T(8,128)(2,1)S(1)}, bf16[1280,128]{1,0:T(8,128)(2,1)S(1)}, u32[]{:S(2)}, u32[]{:S(2)}) collective-permute-start(bf16[1280,128]{1,0:T(8,128)(2,1)S(1)} %get-tuple-element.25), channel_id=1, source_target_pairs={{0,4},{4,8},{8,12},{12,0},{1,5},{5,9},{9,13},{13,1},{2,6},{6,10},{... | collective-permute-start | bytes 983048 | tf_op jit(solution)/shard_map/ppermute | solution.py:19
  1.4 1.3 %collective-permute-start.3 = (bf16[256,128]{1,0:T(8,128)(2,1)S(1)}, bf16[256,128]{1,0:T(8,128)(2,1)S(1)}, u32[]{:S(2)}, u32[]{:S(2)}) collective-permute-start(bf16[256,128]{1,0:T(8,128)(2,1)S(1)} %get-tuple-element.26), channel_id=1, source_target_pairs={{0,8},{4,12},{1,9},{5,13},{2,10},{6,14},{3,11},{7,15},{16,24},{20,... | collective-permute-start | bytes 196616 | tf_op jit(solution)/shard_map/ppermute | solution.py:24
  2.7 1.3 %collective-permute-start.2 = (bf16[256,128]{1,0:T(8,128)(2,1)S(1)}, bf16[256,128]{1,0:T(8,128)(2,1)S(1)}, u32[]{:S(2)}, u32[]{:S(2)}) collective-permute-start(bf16[256,128]{1,0:T(8,128)(2,1)S(1)} %get-tuple-element.26), channel_id=1, source_target_pairs={{0,12},{1,13},{2,14},{3,15},{16,28},{17,29},{18,30},{19,31}} | collective-permute-start | bytes 196616 | tf_op jit(solution)/shard_map/ppermute | solution.py:24
  4.0 1.5 %shard_map.56 = (bf16[768,128]{1,0:T(8,128)(2,1)S(1)}, s32[1,4]{1,0:T(1,128)S(4)}, bf16[1024,896]{1,0:T(8,128)(2,1)S(1)}) custom-call(s32[1,2]{1,0:T(1,128)S(4)} %get-tuple-element.19.vert, s32[1,4]{1,0:T(1,128)} %offs_hbm.1, bf16[1024,896]{1,0:T(8,128)(2,1)} %q_hbm.1, bf16[2048,128]{1,0:T(8,128)(2,1)S(1)} %get-tuple-element.20.kw.k_win.refs_3_, ...), custom_call_target="tpu_custom_call" | custom-call | flops 1000000 | bytes 1048576 | tf_op jit(solution)/shard_map/pallas_call | solution.py:295
  5.5 4.8 %collective-permute-start = (bf16[768,128]{1,0:T(8,128)(2,1)S(1)}, bf16[768,128]{1,0:T(8,128)(2,1)S(1)}, u32[]{:S(2)}, u32[]{:S(2)}) collective-permute-start(bf16[768,128]{1,0:T(8,128)(2,1)S(1)} %get-tuple-element.24), channel_id=1, source_target_pairs={{0,4},{4,8},{8,12},{12,0},{1,5},{5,9},{9,13},{13,1},{2,6},{6,10},{... | collective-permute-start | bytes 589832 | tf_op jit(solution)/shard_map/ppermute | solution.py:19
  10.3 0.1 shard_map.57.refs_2_
  10.5 5.4 %collective-permute-done.3.refs_1_ = bf16[256,128]{1,0:T(8,128)(2,1)S(1)} collective-permute-done((bf16[256,128]{1,0:T(8,128)(2,1)S(1)}, bf16[256,128]{1,0:T(8,128)(2,1)S(1)}, u32[]{:S(2)}, u32[]{:S(2)}) %collective-permute-start.3) | collective-permute-done | bytes 65568 | tf_op jit(solution)/shard_map/ppermute | solution.py:24
  15.8 0.0 collective-permute-done.2.refs_0_
  15.8 0.0 collective-permute-done.1.early
  15.8 4.4 %shard_map.58 = (bf16[1024,896]{1,0:T(8,128)(2,1)}, bf16[2048,128]{1,0:T(8,128)(2,1)S(1)}, bf16[2048,128]{1,0:T(8,128)(2,1)S(1)}, bf16[256,128]{1,0:T(8,128)(2,1)S(1)}, bf16[256,128]{1,0:T(8,128)(2,1)S(1)}) custom-call(s32[1,4]{1,0:T(1,128)S(4)} %get-tuple-element.22.offs, ...), custom_call_target="tpu_custom_call", output_to_operand_aliasing={{0}: (6, {}), {1}: (7, {}), {2}: (8, {})} | custom-call | flops 3000000000 | bytes 1048576 | tf_op jit(solution)/shard_map/pallas_call | solution.py:321
  20.2 0.0 collective-permute-done.late
  20.2 4.3 %shard_map.59 = (bf16[1024,896]{1,0:T(8,128)(2,1)}, bf16[2048,128]{1,0:T(8,128)(2,1)S(1)}, bf16[2048,128]{1,0:T(8,128)(2,1)S(1)}) custom-call(s32[1,4]{1,0:T(1,128)S(4)} %get-tuple-element.22.offs, s32[1,2]{1,0:T(1,128)S(4)} %get-tuple-element.19.vert, ...), custom_call_target="tpu_custom_call", output_to_operand_aliasing={{0}: (6, {}), {1}: (7, {}), {2}: (8, {})} | custom-call | flops 1000000 | bytes 1048576 | tf_op jit(solution)/shard_map/pallas_call | solution.py:330
Async XLA Ops:
  1.1 14.8 %collective-permute-start.1 = (bf16[1280,128]{1,0:T(8,128)(2,1)S(1)}, bf16[1280,128]{1,0:T(8,128)(2,1)S(1)}, u32[]{:S(2)}, u32[]{:S(2)}) collective-permute-start(bf16[1280,128]{1,0:T(8,128)(2,1)S(1)} %get-tuple-element.25), channel_id=1, source_target_pairs={{0,4},{4,8},{8,12},{12,0},{1,5},{5,9},{9,13},{13,1},{2,6},{6,10},{... | collective-permute-start | bytes 983048 | tf_op jit(solution)/shard_map/ppermute | solution.py:19
  1.4 14.5 %collective-permute-start.3 = (bf16[256,128]{1,0:T(8,128)(2,1)S(1)}, bf16[256,128]{1,0:T(8,128)(2,1)S(1)}, u32[]{:S(2)}, u32[]{:S(2)}) collective-permute-start(bf16[256,128]{1,0:T(8,128)(2,1)S(1)} %get-tuple-element.26), channel_id=1, source_target_pairs={{0,8},{4,12},{1,9},{5,13},{2,10},{6,14},{3,11},{7,15},{16,24},{20,... | collective-permute-start | bytes 196616 | tf_op jit(solution)/shard_map/ppermute | solution.py:24
  2.7 13.2 %collective-permute-start.2 = (bf16[256,128]{1,0:T(8,128)(2,1)S(1)}, bf16[256,128]{1,0:T(8,128)(2,1)S(1)}, u32[]{:S(2)}, u32[]{:S(2)}) collective-permute-start(bf16[256,128]{1,0:T(8,128)(2,1)S(1)} %get-tuple-element.26), channel_id=1, source_target_pairs={{0,12},{1,13},{2,14},{3,15},{16,28},{17,29},{18,30},{19,31}} | collective-permute-start | bytes 196616 | tf_op jit(solution)/shard_map/ppermute | solution.py:24
  5.5 14.7 %collective-permute-start = (bf16[768,128]{1,0:T(8,128)(2,1)S(1)}, bf16[768,128]{1,0:T(8,128)(2,1)S(1)}, u32[]{:S(2)}, u32[]{:S(2)}) collective-permute-start(bf16[768,128]{1,0:T(8,128)(2,1)S(1)} %get-tuple-element.24), channel_id=1, source_target_pairs={{0,4},{4,8},{8,12},{12,0},{1,5},{5,9},{9,13},{13,1},{2,6},{6,10},{... | collective-permute-start | bytes 589832 | tf_op jit(solution)/shard_map/ppermute | solution.py:19
